TPU v7x, 512 devices: a whole 4x8x8 slice. The times are simulated.
512 devices in a mesh: node: 32 (over z, x), ens: 4 (over y_lo), dp: 4 (over y_hi, core).
Axes of the slice: x: 4, y: 8 (y_hi: 2, y_lo: 4; y = y_hi * 4 + y_lo), z: 8, core: 2. Of those that a mesh axis runs over, the one named last changes fastest.
Arguments:
- nodes: bfloat16 [4, 4, 4096, 1024], P('dp', 'ens', 'node'), may hold values from -6 to 6
- w_query: bfloat16 [1024, 1024], P('node'), may hold values from -0.1875 to 0.1875
- w_key: bfloat16 [1024, 1024], P('node'), may hold values from -0.1875 to 0.1875
- w_value: bfloat16 [1024, 1024], P('node'), may hold values from -0.1875 to 0.1875
- w_output: bfloat16 [1024, 1024], P('node'), may hold values from -0.1875 to 0.1875
- w_head: bfloat16 [1024, 128], P('node'), may hold values from -0.25 to 0.25
- neighbours: int32 [4096, 16], P('node'), may hold values from 0 to 4095, as said below
- edge_counts: int32 [4096], P('node'), may hold values from 1 to 16
- target: float32 [4, 4096, 128], P('dp', 'node'), may hold values from -6 to 6
- node_area: float32 [4096], P('node'), may hold values from 1 to 10
Outputs:
- grad_nodes: bfloat16 [4, 4, 4096, 1024], P('dp', 'ens', 'node')
- grad_out_proj: float32 [1048576], P(('node', 'ens', 'dp'))
Inputs may be any that keep to these rules, and one draw needn't show every extreme that they name: `neighbours`: row i lists 16 different nodes: slot 0 is i itself and every other slot is (i + o) mod 4096 with 1 <= |o| <= 32. Slot s of node i's list is an edge where s < edge_counts[i].
All inputs are finite; a program needn't handle non-finite values.
Results may differ from a plain program's by a relative error of at most 0.015.
Values may be sent and summed in bfloat16 or wider, within the bound.
A program may use at most 64 MiB of HBM per device.

v0:
```python
import math

import jax
import jax.numpy as jnp
from jax import lax
from jax.sharding import PartitionSpec as P

HEADS = 16


fair_weight = 0.95
soft_square = 0.25


def padded(block, sides, width):
    for axis, dim in sides:
        count = lax.axis_size(axis)
        forward = [(i, i + 1) for i in range(count - 1)]
        forward.append((count - 1, 0))
        backward = [(target, source) for source, target in forward]
        low = lax.ppermute(
            lax.slice_in_dim(block, block.shape[dim] - width, None, axis=dim), axis, forward
        )
        high = lax.ppermute(lax.slice_in_dim(block, 0, width, axis=dim), axis, backward)
        block = jnp.concatenate([low, block, high], axis=dim)
    return block


def passed_along(block, axis, distance):
    devices = range(lax.axis_size(axis))
    route = [((i - distance) % len(devices), i) for i in devices]
    return lax.ppermute(block, axis, route)


def layer_norm(inputs):
    values = inputs.astype(jnp.float32)
    centre = jnp.mean(values, axis=-1, keepdims=True)
    shifted = values - centre
    factor = lax.rsqrt(jnp.mean(shifted * shifted, axis=-1, keepdims=True) + 1e-05)
    return (shifted * factor, factor)


def layer_norm_back(grad_in, normal, factor):
    centre = jnp.mean(grad_in, axis=-1, keepdims=True)
    along = jnp.mean(grad_in * normal, axis=-1, keepdims=True)
    return factor * (grad_in - centre - normal * along)


def head_norm(values, head_count):
    grouped = values.reshape(values.shape[0], head_count, values.shape[1] // head_count)
    factor = lax.rsqrt(jnp.mean(grouped * grouped, axis=-1, keepdims=True) + 1e-06)
    return (grouped * factor, factor)


def head_norm_back(grad_in, normal, factor):
    along = jnp.mean(grad_in * normal, axis=-1, keepdims=True)
    return factor * (grad_in - normal * along)


def soft_sign(values):
    return values * lax.rsqrt(values * values + soft_square)


def matmul(left, right):
    return jnp.dot(left, right, preferred_element_type=jnp.float32)


def matmul_back(left, right):
    return lax.dot_general(
        left, right, (((1,), (1,)), ((), ())), preferred_element_type=jnp.float32
    )


def shards(
    nodes, w_query, w_key, w_value, w_output, w_head, neighbours, edge_counts, target, node_area
):
    model_width = nodes.shape[3]
    local_rows = nodes.shape[2]
    head_size = model_width // HEADS
    reach_rows = local_rows // 4
    extended = local_rows + 2 * reach_rows
    w_query, w_key, w_value, w_output, w_head = (
        lax.all_gather(w_query, "node", axis=0, tiled=True),
        lax.all_gather(w_key, "node", axis=0, tiled=True),
        lax.all_gather(w_value, "node", axis=0, tiled=True),
        lax.all_gather(w_output, "node", axis=0, tiled=True),
        lax.all_gather(w_head, "node", axis=0, tiled=True),
    )
    graph_nodes = nodes[0, 0]
    normal, factor = layer_norm(graph_nodes)
    normed = normal.astype(jnp.bfloat16)
    query_unit, query_factor = head_norm(matmul(normed, w_query), HEADS)
    key_unit, key_factor = head_norm(matmul(normed, w_key), HEADS)
    query_half = query_unit.astype(jnp.bfloat16)
    key_flat = key_unit.astype(jnp.bfloat16).reshape(local_rows, model_width)
    value_flat = matmul(normed, w_value).astype(jnp.bfloat16)
    stacked = jnp.stack((key_flat, value_flat), axis=1)
    widened = padded(stacked, (("node", 0),), reach_rows)
    key_ext = widened[:, 0]
    value_ext = widened[:, 1]
    key_ext = key_ext.reshape(extended, HEADS, head_size)
    value_ext = value_ext.reshape(extended, HEADS, head_size)
    node_count = local_rows * lax.axis_size("node")
    first_row = lax.axis_index("node") * local_rows
    columns = (neighbours - first_row + reach_rows) % node_count
    slot_valid = jnp.arange(neighbours.shape[1], dtype=jnp.int32)[None, :] < edge_counts[:, None]
    hits = (
        columns[:, :, None] == jnp.arange(extended, dtype=jnp.int32)[None, None, :]
    ) & slot_valid[:, :, None]
    adjacency = jnp.sum(hits.astype(jnp.float32), axis=1)
    group_size = max(1, HEADS // 4)
    group_total = HEADS // group_size
    kept_weights = []
    kept_halves = []
    mixed_parts = []
    for head_group in range(group_total):
        head_first = head_group * group_size
        head_last = head_first + group_size
        scores = jnp.einsum(
            "ihd,jhd->hij",
            query_half[:, head_first:head_last],
            key_ext[:, head_first:head_last],
            preferred_element_type=jnp.float32,
        ) / math.sqrt(head_size)
        raised = jnp.exp(scores) * adjacency[None]
        attention = raised / jnp.sum(raised, axis=-1, keepdims=True)
        attention_half = attention.astype(jnp.bfloat16)
        mixed_parts.append(
            jnp.einsum(
                "hij,jhd->ihd",
                attention_half,
                value_ext[:, head_first:head_last],
                preferred_element_type=jnp.float32,
            ).astype(jnp.bfloat16)
        )
        kept_weights.append(attention)
        kept_halves.append(attention_half)
    mixed = jnp.concatenate(mixed_parts, axis=1).reshape(local_rows, model_width)
    settled = (graph_nodes.astype(jnp.float32) + matmul(mixed, w_output)).astype(jnp.bfloat16)
    predicted = matmul(settled, w_head)
    differ = predicted - target[0]
    members = lax.axis_size("ens")
    coefficient = fair_weight / (2 * members * (members - 1)) + (1 - fair_weight) / (
        2 * members * members
    )
    every = lax.all_gather(differ[None], "ens", axis=0, tiled=True)
    paired = jnp.zeros_like(differ)
    for other in range(members):
        paired = paired + soft_sign(differ - every[other])
    core = soft_sign(differ) / members - 2 * coefficient * paired
    grad_pred = (node_area[:, None] * core).astype(jnp.bfloat16)
    grad_settled = matmul_back(grad_pred, w_head).astype(jnp.bfloat16)
    out_grad = lax.dot_general(
        mixed, grad_settled, (((0,), (0,)), ((), ())), preferred_element_type=jnp.float32
    )
    grad_out_proj = lax.psum_scatter(
        out_grad.reshape(-1), ("node", "ens", "dp"), scatter_dimension=0, tiled=True
    )
    grad_mixed = (
        matmul_back(grad_settled, w_output)
        .astype(jnp.bfloat16)
        .reshape(local_rows, HEADS, head_size)
    )
    query_parts = []
    key_parts = []
    value_parts = []
    for head_group in range(group_total):
        head_first = head_group * group_size
        head_last = head_first + group_size
        attention = kept_weights[head_group]
        attention_half = kept_halves[head_group]
        grad_group = grad_mixed[:, head_first:head_last]
        grad_scores = jnp.einsum(
            "ihd,jhd->hij",
            grad_group,
            value_ext[:, head_first:head_last],
            preferred_element_type=jnp.float32,
        )
        grad_logits = (
            attention * (grad_scores - jnp.sum(attention * grad_scores, axis=-1, keepdims=True))
        ).astype(jnp.bfloat16)
        value_parts.append(
            jnp.einsum(
                "hij,ihd->jhd", attention_half, grad_group, preferred_element_type=jnp.float32
            )
        )
        query_parts.append(
            jnp.einsum(
                "hij,jhd->ihd",
                grad_logits,
                key_ext[:, head_first:head_last],
                preferred_element_type=jnp.float32,
            )
            / math.sqrt(head_size)
        )
        key_parts.append(
            jnp.einsum(
                "hij,ihd->jhd",
                grad_logits,
                query_half[:, head_first:head_last],
                preferred_element_type=jnp.float32,
            )
            / math.sqrt(head_size)
        )
    key_grad_ext = jnp.concatenate(key_parts, axis=1).reshape(extended, model_width)
    value_grad_ext = jnp.concatenate(value_parts, axis=1).reshape(extended, model_width)
    stacked_grad = jnp.stack((key_grad_ext, value_grad_ext), axis=1)
    from_lower = passed_along(
        stacked_grad[extended - reach_rows :].astype(jnp.bfloat16), "node", 1
    ).astype(jnp.float32)
    from_upper = passed_along(stacked_grad[:reach_rows].astype(jnp.bfloat16), "node", -1).astype(
        jnp.float32
    )
    local_grad = stacked_grad[reach_rows : reach_rows + local_rows]
    local_grad = local_grad.at[:reach_rows].add(from_lower)
    local_grad = local_grad.at[local_rows - reach_rows :].add(from_upper)
    query_grad = jnp.concatenate(query_parts, axis=1)
    grad_query = (
        head_norm_back(query_grad, query_unit, query_factor)
        .astype(jnp.bfloat16)
        .reshape(local_rows, model_width)
    )
    key_grad = local_grad[:, 0].reshape(local_rows, HEADS, head_size)
    grad_key = (
        head_norm_back(key_grad, key_unit, key_factor)
        .astype(jnp.bfloat16)
        .reshape(local_rows, model_width)
    )
    grad_value = local_grad[:, 1].astype(jnp.bfloat16)
    grad_normed = (
        matmul_back(grad_query, w_query)
        + matmul_back(grad_key, w_key)
        + matmul_back(grad_value, w_value)
    )
    grad_nodes = (
        grad_settled.astype(jnp.float32) + layer_norm_back(grad_normed, normal, factor)
    ).astype(jnp.bfloat16)
    return (grad_nodes.reshape(nodes.shape), grad_out_proj)


def solution(mesh):
    placed = (
        P("dp", "ens", "node", None),
        P("node", None),
        P("node", None),
        P("node", None),
        P("node", None),
        P("node", None),
        P("node", None),
        P("node"),
        P("dp", "node", None),
        P("node"),
    )
    return jax.shard_map(
        shards,
        mesh=mesh,
        in_specs=placed,
        out_specs=(P("dp", "ens", "node", None), P(("node", "ens", "dp"))),
        check_vma=False,
    )
```

profile of v0, /device:TPU:1, one launch (start us, length us, event | category | flops | bytes accessed | tf_op | source)
XLA Modules:
  0.0 696.6 jit_solution(10782600176253186834)
XLA Ops:
  7.2 0.7 all-gather.6.cloned.1.call-update
  7.9 0.7 all-gather.10.cloned.1.call-update
  8.7 0.7 all-gather.8.cloned.1.call-update
  9.4 0.5 all-gather.12.cloned.1.call-update
  10.0 1.1 convert_reduce_fusion.1
  11.1 1.2 fusion.40
  12.3 49.2 %all_gather.22 = bf16[1024,128]{1,0:T(8,128)(2,1)} all-gather(bf16[32,128]{1,0:T(8,128)(2,1)} %param.19), channel_id=1, replica_groups=mesh['node'=32,'ens'=4,'dp'=4] {'node'}, dimensions={0}, use_global_device_ids=true | all-gather | bytes 270336 | tf_op jit(solution)/shard_map/all_gather | solution.py:87
  61.5 0.7 iota_compare_fusion.1
  62.1 0.7 add_select_fusion
  63.1 33.6 %all-gather.6.cloned.1.call-done = bf16[1024,1024]{1,0:T(8,128)(2,1)} async-done(((bf16[32,1024]{1,0:T(8,128)(2,1)}), bf16[1024,1024]{1,0:T(8,128)(2,1)}) %all-gather.6.cloned.1.call-update) | async-done | bytes 2097168 | tf_op jit(solution)/shard_map/all_gather | solution.py:84
  96.7 2.9 copy.42
  99.6 0.8 multiply_reduce_fusion.3
  100.4 80.3 %all-gather.10.cloned.1.call-done = bf16[1024,1024]{1,0:T(8,128)(2,1)} async-done(((bf16[32,1024]{1,0:T(8,128)(2,1)}), bf16[1024,1024]{1,0:T(8,128)(2,1)}) %all-gather.10.cloned.1.call-update) | async-done | bytes 2097168 | tf_op jit(solution)/shard_map/all_gather | solution.py:83
  180.7 2.9 copy.45
  183.8 80.9 %all-gather.8.cloned.1.call-done = bf16[1024,1024]{1,0:T(8,128)(2,1)} async-done(((bf16[32,1024]{1,0:T(8,128)(2,1)}), bf16[1024,1024]{1,0:T(8,128)(2,1)}) %all-gather.8.cloned.1.call-update) | async-done | bytes 2097168 | tf_op jit(solution)/shard_map/all_gather | solution.py:85
  264.8 2.1 fusion.12
  266.9 3.9 collective-permute-start.1
  270.8 1.9 collective-permute-start
  272.8 0.8 multiply_reduce_fusion.2
  273.6 0.8 copy-done.5
  274.4 5.4 collective-permute-done
  280.9 0.3 fusion.8
  281.5 0.3 fusion.7
  282.6 0.4 copy-done.21
  283.1 65.5 %all-gather.12.cloned.1.call-done = bf16[1024,1024]{1,0:T(8,128)(2,1)} async-done(((bf16[32,1024]{1,0:T(8,128)(2,1)}), bf16[1024,1024]{1,0:T(8,128)(2,1)}) %all-gather.12.cloned.1.call-update) | async-done | bytes 2097168 | tf_op jit(solution)/shard_map/all_gather | solution.py:86
  348.6 2.4 fusion.21
  351.0 11.4 %all-gather = f32[512,128]{1,0:T(8,128)S(1)} all-gather(f32[128,128]{1,0:T(8,128)S(1)} %fusion.21), channel_id=2, replica_groups=mesh['node'=32,'ens'=4,'dp'=4] {'ens'}, dimensions={0}, use_global_device_ids=true | all-gather | bytes 327680 | tf_op jit(solution)/shard_map/all_gather | solution.py:146
  362.4 1.2 convolution_convert_fusion.1
  363.6 1.5 convolution_convert_fusion
  365.2 1.1 copy.47
  366.3 1.2 fusion.58
  367.5 1.2 fusion.60
  368.7 1.2 fusion.62
  369.9 1.2 fusion.64
  371.1 0.3 multiply_reduce_fusion.4
  371.6 1.0 fusion.13
  372.6 0.3 multiply_reduce_fusion.5
  373.6 0.3 multiply_reduce_fusion.6
  374.6 0.3 multiply_reduce_fusion.7
  375.2 1.0 fusion.16
  376.1 2.1 convolution_bitcast_fusion.1
  378.2 2.1 convolution_bitcast_fusion.2
  380.3 2.1 convolution_bitcast_fusion.3
  382.5 2.1 convolution_bitcast_fusion.4
  384.6 0.7 convolution_bitcast_fusion
  385.3 0.3 copy-done.6
  385.9 0.7 copy-done.13
  387.2 1.2 fusion.97
  388.4 2.1 collective-permute-start.2
  390.5 6.7 collective-permute-start.3
  397.2 3.0 copy.48
  400.2 3.2 fusion.99
  403.4 0.3 fusion.26
  403.8 2.4 fusion.28
  406.2 7.7 %scatter-add.6 = f32[128,2,1024]{0,2,1:T(8,128)S(1)} dynamic-update-slice(f32[128,2,1024]{0,2,1:T(8,128)S(1)} %fusion.26, f32[32,2,1024]{0,2,1:T(8,128)} %fusion.28, s32[]{:T(128)} %constant.113.clone.1, s32[]{:T(128)} %constant.113.clone.1, s32[]{:T(128)} %constant.113.clone.1) | dynamic-update-slice | bytes 524292 | tf_op jit(solution)/shard_map/scatter-add | solution.py:215
  413.9 1.4 slice_add_fusion
  415.3 6.2 scatter-add.9
  421.5 1.3 multiply_reduce_fusion
  422.9 1.3 multiply_convert_fusion
  424.2 0.8 convolution_add_fusion.1
  425.1 1.0 fusion.96
  426.1 1.0 fusion.46
  427.1 261.7 %all-reduce.3.cloned.1.call-done = f32[1048576]{0:T(1024)} async-done(((f32[1048576]{0:T(1024)}), f32[1048576]{0:T(1024)}) %all-reduce.3.cloned.1.call-update) | async-done | bytes 4194320
  688.8 1.3 dynamic-slice.16
  (108 shorter events, 5.7 us)
Async XLA Ops:
  7.2 89.5 %all-gather.6.cloned.1.call-start = ((), (), s32[]{:S(2)}) async-start(), calls=%async_computation | async-start | bytes 2162688 | tf_op jit(solution)/shard_map/all_gather | solution.py:84
  7.9 172.8 %all-gather.10.cloned.1.call-start = ((), (), s32[]{:S(2)}) async-start(), calls=%async_computation.2 | async-start | bytes 2162688 | tf_op jit(solution)/shard_map/all_gather | solution.py:83
  8.6 256.1 %all-gather.8.cloned.1.call-start = ((), (), s32[]{:S(2)}) async-start(), calls=%async_computation.1 | async-start | bytes 2162688 | tf_op jit(solution)/shard_map/all_gather | solution.py:85
  9.4 339.2 %all-gather.12.cloned.1.call-start = ((), (), s32[]{:S(2)}) async-start(), calls=%async_computation.3 | async-start | bytes 2162688 | tf_op jit(solution)/shard_map/all_gather | solution.py:86
  10.0 678.8 %all-reduce.3.cloned.1.call-start = ((), (), s32[]{:S(2)}) async-start(), calls=%async_computation.4 | async-start | bytes 8388608
  11.1 261.7 %copy-start.28 = (f32[128]{0:T(128)}, f32[128]{0:T(128)S(1)}, u32[]{:S(2)}) copy-start(f32[128]{0:T(128)S(1)} %broadcast_multiply_fusion.4) | copy-start | bytes 1540
  12.3 260.5 %copy-start.30 = (f32[128]{0:T(128)}, f32[128]{0:T(128)S(1)}, u32[]{:S(2)}) copy-start(f32[128]{0:T(128)S(1)} %add_rsqrt_fusion.2) | copy-start | bytes 1540
  96.7 2.9 copy-start
  100.4 83.2 %copy-start.4 = (f32[128,16,64]{0,2,1:T(8,128)}, f32[128,16,64]{0,2,1:T(8,128)S(1)}, u32[]{:S(2)}) copy-start(f32[128,16,64]{0,2,1:T(8,128)S(1)} %get-tuple-element.35) | copy-start | bytes 1572868
  266.9 7.6 %collective-permute-start.1 = (bf16[32,2,1024]{2,0,1:T(8,128)(2,1)S(1)}, bf16[32,2,1024]{2,0,1:T(8,128)(2,1)S(1)}, u32[]{:S(2)}, u32[]{:S(2)}) collective-permute-start(bf16[32,2,1024]{2,0,1:T(8,128)(2,1)S(1)} %get-tuple-element.33), channel_id=1, source_target_pairs={{16,0},{32,16},{48,32},{64,48},{80,64},{96,80},{112,96},{128,112},... | collective-permute-start | bytes 393224 | tf_op jit(solution)/shard_map/ppermute | solution.py:24
  270.8 9.0 %collective-permute-start = (bf16[32,2,1024]{2,0,1:T(8,128)(2,1)S(1)}, bf16[32,2,1024]{2,0,1:T(8,128)(2,1)S(1)}, u32[]{:S(2)}, u32[]{:S(2)}) collective-permute-start(bf16[32,2,1024]{2,0,1:T(8,128)(2,1)S(1)} %get-tuple-element.32), channel_id=1, source_target_pairs={{0,16},{16,32},{32,48},{48,64},{64,80},{80,96},{96,112},{112,128},... | collective-permute-start | bytes 393224 | tf_op jit(solution)/shard_map/ppermute | solution.py:21
  273.6 0.8 copy-start.5
  280.4 1.9 copy-start.11
  280.7 0.8 copy-start.15
  281.2 0.8 copy-start.17
  281.8 0.8 copy-start.19
  281.8 66.9 %copy-start.27 = (f32[1,128,128]{2,1,0:T(8,128)S(1)}, f32[1,128,128]{2,1,0:T(8,128)}, u32[]{:S(2)}) copy-start(f32[1,128,128]{2,1,0:T(8,128)} %param.22) | copy-start | bytes 196612
  282.3 0.7 copy-start.21
  283.1 67.9 %copy-start.9 = (bf16[128,16,64]{0,2,1:T(8,128)(2,1)}, bf16[128,16,64]{0,2,1:T(8,128)(2,1)S(1)}, u32[]{:S(2)}) copy-start(bf16[128,16,64]{0,2,1:T(8,128)(2,1)S(1)} %pad_maximum_fusion.5) | copy-start | bytes 786436
  348.6 15.0 %copy-start.2 = (bf16[1024,1024]{1,0:T(8,128)(2,1)S(1)}, bf16[1024,1024]{1,0:T(8,128)(2,1)}, u32[]{:S(2)}) copy-start(bf16[1024,1024]{1,0:T(8,128)(2,1)} %all-gather.12.cloned.1.call-done) | copy-start | bytes 6291460
  363.6 21.0 %copy-start.7 = (bf16[128,1024]{1,0:T(8,128)(2,1)}, bf16[128,1024]{1,0:T(8,128)(2,1)S(1)}, u32[]{:S(2)}) copy-start(bf16[128,1024]{1,0:T(8,128)(2,1)S(1)} %convolution_convert_fusion.1) | copy-start | bytes 786436
  366.3 4.8 copy-start.16
  371.0 1.6 copy-start.18
  372.6 1.0 copy-start.20
  373.6 1.0 copy-start.22
  380.3 4.3 copy-start.10
  384.6 1.0 copy-start.6
  385.6 0.9 copy-start.13
  385.6 1.0 copy-start.14
  385.6 1.1 copy-start.23
  385.6 1.2 copy-start.24
  385.7 1.3 copy-start.25
  385.7 1.3 copy-start.26
  388.4 15.3 %collective-permute-start.2 = (bf16[32,2,1024]{0,2,1:T(8,128)(2,1)}, bf16[32,2,1024]{0,2,1:T(8,128)(2,1)}, u32[]{:S(2)}, u32[]{:S(2)}) collective-permute-start(bf16[32,2,1024]{0,2,1:T(8,128)(2,1)} %get-tuple-element.29), channel_id=1, source_target_pairs={{496,0},{0,16},{16,32},{32,48},{48,64},{64,80},{80,96},{96,112},{1... | collective-permute-start | bytes 393224 | tf_op jit(solution)/shard_map/ppermute | solution.py:32
  390.5 23.4 %collective-permute-start.3 = (bf16[32,2,1024]{0,2,1:T(8,128)(2,1)}, bf16[32,2,1024]{0,2,1:T(8,128)(2,1)}, u32[]{:S(2)}, u32[]{:S(2)}) collective-permute-start(bf16[32,2,1024]{0,2,1:T(8,128)(2,1)} %get-tuple-element.28), channel_id=1, source_target_pairs={{16,0},{32,16},{48,32},{64,48},{80,64},{96,80},{112,96},{128,112},... | collective-permute-start | bytes 393224 | tf_op jit(solution)/shard_map/ppermute | solution.py:32
  421.5 2.7 copy-start.3
  421.5 2.7 copy-start.12
  422.8 2.2 copy-start.1
  422.8 2.2 copy-start.29
  422.9 2.2 copy-start.31
  425.1 1.0 copy-start.8
Sparse Core Ops, SparseCore 0:
  11.2 85.4 all-gather.5
  99.8 80.8 all-gather.9
  183.9 80.8 all-gather.7
  267.8 80.8 all-gather.11
  400.3 288.3 all-reduce.2
where the time goes:
time: 699 us; the launch traced here: 697 us
  waiting for transfers between devices  530 us (76%)
  blocking collectives  60.5 us (9%)
  matrix products  32.9 us (5%)
  local copies, waits for them, and re-layouts  29.9 us (4%)
  starting transfers between devices  14.8 us (2%)
  between operations  14.5 us (2%)
  other arithmetic  13.8 us (2%)
    unnamed x6, waiting for transfers between devices  264 us
    all_gather x1, waiting for transfers between devices, shards(): lax.all_gather(w_value, 'node', axis=0, tiled=True)  80.9 us
    all_gather x1, waiting for transfers between devices, shards(): lax.all_gather(w_query, 'node', axis=0, tiled=True)  80.3 us
    all_gather x1, waiting for transfers between devices, shards(): lax.all_gather(w_output, 'node', axis=0, tiled=True)  65.5 us
    all_gather x1, blocking collectives, shards(): lax.all_gather(w_head, 'node', axis=0, tiled=True)  49.2 us
    all_gather x1, waiting for transfers between devices, shards(): lax.all_gather(w_key, 'node', axis=0, tiled=True)  33.6 us
  transfers between devices with their start and end apart: 9, of which 6 were waited for; matrix products, arithmetic and copies ran while one was open for 7% of the time, Pallas kernels for 0%

commit v1 on v0

v1 whole, which is shorter than its diff:
```python
import jax
import jax.numpy as jnp
from jax import lax
from jax.experimental import pallas as pl
from jax.experimental.pallas import tpu as pltpu
from jax.sharding import PartitionSpec as P

HEADS = 16


fair_weight = 0.95
soft_square = 0.25

NZ, NX, NY = 8, 4, 8
MESH = pl.DeviceIdType.MESH


def place():
    node = lax.axis_index("node")
    ens = lax.axis_index("ens")
    dp = lax.axis_index("dp")
    return node // NX, node % NX, (dp // 2) * 4 + ens, dp % 2


def at(z, x, y, core):
    return {"node": z * NX + x, "ens": y % 4, "dp": (y // 4) * 2 + core}


class Sender:
    def __init__(self, sems):
        self.sems, self.count, self.sent = sems, 0, []

    def start(self, src, dst, recv_sem, device):
        copy = pltpu.make_async_remote_copy(
            src_ref=src,
            dst_ref=dst,
            send_sem=self.sems.at[self.count],
            recv_sem=recv_sem,
            device_id=device,
            device_id_type=MESH,
        )
        self.count += 1
        copy.start()
        self.sent.append(copy)

    def finish(self):
        for copy in self.sent:
            copy.wait_send()
        self.sent = []


def landed(region, sem):
    pltpu.make_async_copy(region, region, sem).wait()


def greet(peers):
    barrier = pltpu.get_barrier_semaphore()
    for peer in peers:
        pl.semaphore_signal(barrier, inc=1, device_id=peer, device_id_type=MESH)
    pl.semaphore_wait(barrier, len(peers))


TILE = 256
HALO = 32
EXT = 256
FIRST = 1024


def spread(z):
    return (z + 2 * NZ) % NZ


class Gather:
    def __init__(self, whole, sender, recv, pair):
        self.whole, self.sender, self.recv, self.pair = whole, sender, recv, pair
        self.z, self.x, self.y, self.core = place()
        z, x, y, core = self.z, self.x, self.y, self.core
        self.half = pl.ds(pl.multiple_of(core * 16, 16), 16)
        self.near = [at(z, (x + d) % NX, y, core) for d in (1, 2, 3)]
        self.up = at((z + 1) % NZ, x, y, core)
        self.down = at((z + NZ - 1) % NZ, x, y, core)
        self.twin = at(z, x, y, 1 - core)

    def send(self, region, sem, peer):
        self.sender.start(region, region, self.recv.at[sem], peer)

    def share(self, region):
        self.sender.start(region, region, self.pair, self.twin)

    def paired(self):
        landed(self.whole.at[:, :, pl.ds(0, 16)], self.pair)

    def own(self, columns):
        return self.whole.at[self.z, self.x, self.half, columns]

    def line(self, dz, columns):
        return self.whole.at[spread(self.z + dz), :, self.half, columns]

    def one(self, dz, columns):
        return self.whole.at[spread(self.z + dz), self.x, self.half, columns]

    def across(self, columns, base):
        for d in range(3):
            self.send(self.own(columns), base + d, self.near[d])

    def crossed(self, columns, base):
        for d in (1, 2, 3):
            region = self.whole.at[
                self.z, (self.x - d + NX) % NX, self.half, columns
            ]
            landed(region, self.recv.at[base + d - 1])

    def pass_crossed(self, columns):
        for d in (1, 2, 3):
            self.share(
                self.whole.at[self.z, (self.x - d + NX) % NX, self.half, columns]
            )

    def ring_begin(self, block, columns, base):
        self.send(block(0, columns), base, self.up)
        self.send(block(0, columns), base + 4, self.down)

    def ring_step(self, block, columns, base, s, shared=True):
        low, high = block(-s, columns), block(s, columns)
        landed(low, self.recv.at[base + s - 1])
        if s < 4:
            self.send(low, base + s, self.up)
            landed(high, self.recv.at[base + s + 3])
            if s < 3:
                self.send(high, base + s + 4, self.down)
        if shared:
            self.share(low)
            if s < 4:
                self.share(high)

    def column(self, dx, z0, count, columns):
        x = (self.x + dx + NX) % NX
        return self.whole.at[pl.ds(z0, count), x, self.half, columns]

    def column_begin(self, columns, base):
        region = self.column(0, 0, NZ, columns)
        self.send(region, base, self.near[0])
        self.send(region, base + 1, self.near[2])

    def column_step(self, columns, base):
        for sem, dx, z0, peer in (
            (base, -1, 0, self.near[0]),
            (base + 1, 1, 4, self.near[2]),
        ):
            region = self.column(dx, 0, NZ, columns)
            landed(region, self.recv.at[sem])
            self.send(self.column(dx, z0, 4, columns), sem + 2, peer)
            self.share(region)

    def column_end(self, columns, base):
        for sem, z0 in ((base + 2, 0), (base + 3, 4)):
            region = self.column(2, z0, 4, columns)
            landed(region, self.recv.at[sem])
            self.share(region)

    def slab(self, dy):
        width = self.whole.shape[3] // NY
        first = pl.multiple_of(((self.y + dy + NY) % NY) * width, width)
        return self.whole.at[:, :, self.half, pl.ds(first, width)]

    def y_begin(self, base):
        self.share(self.slab(0))
        y, core = self.y, self.core
        self.send(self.slab(0), base, at(self.z, self.x, (y + 1) % NY, core))
        self.send(self.slab(0), base + 4, at(self.z, self.x, (y + NY - 1) % NY, core))

    def y_step(self, base, s):
        y, core = self.y, self.core
        low, high = self.slab(-s), self.slab(s)
        landed(low, self.recv.at[base + s - 1])
        if s < 4:
            self.send(low, base + s, at(self.z, self.x, (y + 1) % NY, core))
            landed(high, self.recv.at[base + s + 3])
            if s < 3:
                self.send(
                    high, base + s + 4, at(self.z, self.x, (y + NY - 1) % NY, core)
                )
        self.share(low)
        if s < 4:
            self.share(high)


def all_peers():
    z, x, y, core = place()
    node = z * NX + x
    peers = [at(z, (x + d) % NX, y, core) for d in range(1, NX)]
    peers += [at((z + d) % NZ, x, y, core) for d in range(1, NZ)]
    for dy in range(NY):
        for dc in range(2):
            if dy or dc:
                peers.append(at(z, x, (y + dy) % NY, (core + dc) % 2))
    peers.append({"node": (node + 1) % (NZ * NX)})
    peers.append({"node": (node + NZ * NX - 1) % (NZ * NX)})
    return peers


def mat(left, right):
    return jnp.dot(left, right, preferred_element_type=jnp.float32)


def mat_back(left, right):
    return lax.dot_general(
        left, right, (((1,), (1,)), ((), ())), preferred_element_type=jnp.float32
    )


def mat_across(left, right):
    return lax.dot_general(
        left, right, (((0,), (0,)), ((), ())), preferred_element_type=jnp.float32
    )


def soft_sign(values):
    return values * lax.rsqrt(values * values + soft_square)


def lane(start, size):
    return pl.ds(pl.multiple_of(start, size), size)


def head_side():
    return lax.broadcasted_iota(jnp.int32, (1, 128), 1) < 64


def head_mean(values):
    side = head_side()
    low = jnp.sum(jnp.where(side, values, 0.0), axis=1, keepdims=True)
    high = jnp.sum(jnp.where(side, 0.0, values), axis=1, keepdims=True)
    return jnp.where(side, low, high) * (1.0 / 64)


def two_heads(values):
    side = head_side()
    empty = jnp.zeros_like(values)
    return jnp.where(side, values, empty), jnp.where(side, empty, values)


def layer_kernel(
    nodes, wq_shard, wk_shard, wv_shard, wo_shard, wh_shard, neighbours, counts,
    target, area, out, out_sum,
    wqkv, wo, wh, normal, normed, factor, q_unit, k_unit, q_factor, k_factor, q_half,
    kv, near, attention, left, right, settled, differ, differs, gs, gm, gq, dk, dv,
    gk, gv, gn, halo_out, halo_in, parts, from_x, halves, from_z, pieces, from_y,
    local, send, recv_a, recv_o, recv_h, pair, halo_send, halo_recv, back_recv,
    ens_recv, recv_core, recv_x, recv_z, recv_y,
):
    f32, half = jnp.float32, jnp.bfloat16
    z, x, y, core = place()
    node = z * NX + x
    rows, width = nodes.shape
    sender = Sender(send)
    own_half = pl.ds(pl.multiple_of(core * 16, 16), 16)
    loads = []
    slab = pl.ds(pl.multiple_of(y * 128, 128), 128)
    all_columns = pl.ds(0, width)
    every_h = pl.ds(0, wh_shard.shape[1])
    for k, (shard, whole, taken, kept) in enumerate(
        (
            (wq_shard, wqkv, all_columns, pl.ds(0, width)),
            (wk_shard, wqkv, all_columns, pl.ds(width, width)),
            (wv_shard, wqkv, all_columns, pl.ds(2 * width, width)),
            (wo_shard, wo, slab, slab),
            (wh_shard, wh, every_h, every_h),
        )
    ):
        load = pltpu.make_async_copy(
            shard.at[own_half, taken],
            whole.at[z, x, own_half, kept],
            local.at[k],
        )
        load.start()
        loads.append(load)
    greet(all_peers())
    for load in loads:
        load.wait()

    ga = Gather(wqkv, sender, recv_a, pair.at[0])
    go = Gather(wo, sender, recv_o, pair.at[1])
    gh = Gather(wh, sender, recv_h, pair.at[2])
    first, last = pl.ds(0, FIRST), pl.ds(FIRST, 3 * width - FIRST)
    ga.across(last, 0)
    ga.ring_begin(ga.one, first, 3)
    go.across(slab, 0)
    gh.across(every_h, 0)
    ga.share(ga.own(pl.ds(0, 3 * width)))
    gh.share(gh.own(every_h))

    values = nodes[...].astype(f32)
    shifted = values - jnp.mean(values, axis=1, keepdims=True)
    scale = lax.rsqrt(jnp.mean(shifted * shifted, axis=1, keepdims=True) + 1e-05)
    factor[...] = jnp.broadcast_to(scale, factor.shape)
    normal[...] = shifted * scale
    normed[...] = normal[...].astype(half)

    ga.crossed(last, 0)
    ga.ring_begin(ga.line, last, 10)
    ga.ring_step(ga.one, first, 3, 1)
    go.crossed(slab, 0)
    go.ring_begin(go.line, slab, 3)
    gh.crossed(every_h, 0)
    gh.ring_begin(gh.line, every_h, 3)
    ga.pass_crossed(last)
    gh.pass_crossed(every_h)

    column = (
        neighbours[...] - node * rows + HALO + NZ * NX * rows
    ) & (NZ * NX * rows - 1)
    at_column = lax.broadcasted_iota(jnp.int32, (rows, EXT), 1)
    hits = jnp.zeros((rows, EXT), f32)
    for s in range(neighbours.shape[1]):
        hit = (column[:, s : s + 1] == at_column) & (counts[...] > s)
        hits = hits + jnp.where(hit, 1.0, 0.0)
    near[...] = hits
    kv[:, pl.ds(rows + 2 * HALO, EXT - rows - 2 * HALO)] = jnp.zeros(
        (2, EXT - rows - 2 * HALO, width), half
    )

    ga.ring_step(ga.one, first, 3, 2)
    go.ring_step(go.line, slab, 3, 1, False)
    ga.ring_step(ga.one, first, 3, 3)
    go.ring_step(go.line, slab, 3, 2, False)
    gh.ring_step(gh.line, every_h, 3, 1)
    ga.ring_step(ga.one, first, 3, 4)
    ga.column_begin(first, 17)
    go.ring_step(go.line, slab, 3, 3, False)
    ga.ring_step(ga.line, last, 10, 1)
    gh.ring_step(gh.line, every_h, 3, 2)
    go.ring_step(go.line, slab, 3, 4, False)
    go.y_begin(10)
    ga.ring_step(ga.line, last, 10, 2)
    gh.ring_step(gh.line, every_h, 3, 3)
    go.y_step(10, 1)
    ga.column_step(first, 17)
    ga.ring_step(ga.line, last, 10, 3)
    gh.ring_step(gh.line, every_h, 3, 4)
    go.y_step(10, 2)
    ga.column_end(first, 17)
    ga.ring_step(ga.line, last, 10, 4)
    ga.paired()

    before, after = (
        {"node": (node + NZ * NX - 1) % (NZ * NX)},
        {"node": (node + 1) % (NZ * NX)},
    )

    def halo(t, way):
        columns = lane(t * TILE, TILE)
        source, target_rows, peer = (
            (HALO, rows + HALO, before),
            (rows, 0, after),
        )[way]
        return pltpu.make_async_remote_copy(
            src_ref=kv.at[:, pl.ds(source, HALO), columns],
            dst_ref=kv.at[:, pl.ds(target_rows, HALO), columns],
            send_sem=halo_send.at[way, t],
            recv_sem=halo_recv.at[way, t],
            device_id=peer,
            device_id_type=MESH,
        )

    @pl.loop(0, width // TILE)
    def _(t):
        def product(base):
            columns = lane(base + t * TILE, TILE)
            return mat(normed[...], wqkv[:, :, :, columns].reshape(width, TILE))

        inner = pl.ds(HALO, rows)
        for base, unit, kept in ((0, q_unit, q_factor), (width, k_unit, k_factor)):
            full = product(base)
            for side in range(TILE // 128):
                part = full[:, side * 128 : side * 128 + 128]
                columns = lane(t * TILE + side * 128, 128)
                scale = lax.rsqrt(head_mean(part * part) + 1e-06)
                unit[:, columns] = part * scale
                kept[:, columns] = scale
                if base:
                    kv[0, inner, columns] = (part * scale).astype(half)
                else:
                    q_half[:, columns] = (part * scale).astype(half)
        kv[1, inner, lane(t * TILE, TILE)] = product(2 * width).astype(half)
        halo(t, 0).start()
        halo(t, 1).start()

    go.y_step(10, 3)

    @pl.loop(0, width // TILE)
    def _(t):
        halo(t, 0).wait()
        halo(t, 1).wait()

    @pl.loop(0, width // 128)
    def _(p):
        columns = lane(p * 128, 128)
        keys, held = kv[0, :, columns], kv[1, :, columns]
        mixed = []
        for side, query in enumerate(two_heads(q_half[:, columns])):
            raised = jnp.exp(mat_back(query, keys) * 0.125) * near[...]
            weight = raised / jnp.sum(raised, axis=1, keepdims=True)
            attention[2 * p + side] = weight
            mixed.append(mat(weight.astype(half), held))
        left[0, :, columns] = jnp.where(head_side(), mixed[0], mixed[1]).astype(half)

    twin = at(z, x, y, 1 - core)
    sender.start(left.at[0], left.at[1], recv_core.at[0], twin)
    go.y_step(10, 4)
    go.paired()
    gh.paired()

    @pl.loop(0, width // TILE)
    def _(t):
        columns = lane(t * TILE, TILE)
        product = mat(left[0], wo[:, :, :, columns].reshape(width, TILE))
        settled[:, columns] = (nodes[:, columns].astype(f32) + product).astype(half)

    error = mat(settled[...], wh[...].reshape(width, wh.shape[3])) - target[...]
    differ[...] = error
    differs[0] = error.astype(half)
    ens = y % 4
    for d in (1, 2, 3):
        peer = {"ens": (ens + d) % 4}
        sender.start(differs.at[0], differs.at[d], ens_recv.at[d - 1], peer)
    own_sign = soft_sign(error)
    paired = jnp.zeros_like(error)
    for d in (1, 2, 3):
        landed(differs.at[d], ens_recv.at[d - 1])
        paired = paired + soft_sign(error - differs[d].astype(f32))
    members = 4
    coefficient = fair_weight / (2 * members * (members - 1)) + (1 - fair_weight) / (
        2 * members * members
    )
    core_grad = own_sign / members - 2 * coefficient * paired
    grad_pred = (area[...] * core_grad).astype(half)

    @pl.loop(0, width // TILE)
    def _(t):
        block = wh[pl.ds(2 * t, 2)].reshape(TILE, wh.shape[3])
        gs[:, lane(t * TILE, TILE)] = mat_back(grad_pred, block).astype(half)

    wide = width // 2
    mine, other = lane(core * wide, wide), lane((1 - core) * wide, wide)
    sender.start(gs.at[:, other], right.at[1], recv_core.at[1], twin)
    right[0] = gs[:, mine]

    @pl.loop(0, width // TILE)
    def _(t):
        block = wo[pl.ds(2 * t, 2)].reshape(TILE, width)
        gm[:, lane(t * TILE, TILE)] = mat_back(gs[...], block).astype(half)

    landed(left.at[1], recv_core.at[0])
    landed(right.at[1], recv_core.at[1])
    tall = width // NZ

    @pl.loop(0, NZ)
    def _(block):
        columns = lane(block * tall, tall)
        total = mat_across(left[0, :, columns], right[0])
        total = total + mat_across(left[1, :, columns], right[1])
        parts[block] = total.astype(half).reshape(parts.shape[1:])

    for d in range(1, NX):
        sender.start(
            parts.at[:, (x + d) % NX],
            from_x.at[d - 1],
            recv_x.at[d - 1],
            at(z, (x + d) % NX, y, core),
        )

    for group in range(2):
        @pl.loop(group * 4, group * 4 + 4)
        def _(p):
            columns = lane(p * 128, 128)
            keys, held = kv[0, :, columns], kv[1, :, columns]
            grads = two_heads(gm[:, columns])
            queries = two_heads(q_half[:, columns])
            logits, halves_of, query_grad = [], [], []
            for side in range(2):
                weight = attention[2 * p + side]
                scores = mat_back(grads[side], held)
                mean = jnp.sum(weight * scores, axis=1, keepdims=True)
                logit = (weight * (scores - mean)).astype(half)
                logits.append(logit)
                halves_of.append(weight.astype(half))
                query_grad.append(mat(logit, keys))
            grad = jnp.where(head_side(), query_grad[0], query_grad[1]) * 0.125
            unit = q_unit[:, columns]
            gq[:, columns] = (
                q_factor[:, columns] * (grad - unit * head_mean(grad * unit))
            ).astype(half)
            key_grad = (
                mat_across(logits[0], queries[0]) + mat_across(logits[1], queries[1])
            ) * 0.125
            value_grad = mat_across(halves_of[0], grads[0]) + mat_across(
                halves_of[1], grads[1]
            )
            for k, (grad, kept) in enumerate(((key_grad, dk), (value_grad, dv))):
                kept[:, columns] = grad[HALO : HALO + rows]
                halo_out[0, k, :, columns] = grad[:HALO].astype(half)
                halo_out[1, k, :, columns] = grad[
                    HALO + rows : 2 * HALO + rows
                ].astype(half)

        columns = pl.ds(group * wide, wide)
        for way, peer in enumerate((before, after)):
            sender.start(
                halo_out.at[way, :, :, columns],
                halo_in.at[way, :, :, columns],
                back_recv.at[way, group],
                peer,
            )

    @pl.loop(0, width // TILE)
    def _(t):
        block = wqkv[pl.ds(2 * t, 2), :, :, pl.ds(0, width)].reshape(TILE, width)
        gn[:, lane(t * TILE, TILE)] = mat_back(gq[...], block)

    for d in range(1, NX):
        landed(from_x.at[d - 1], recv_x.at[d - 1])
    total = parts[:, x].astype(f32)
    for d in range(1, NX):
        total = total + from_x[d - 1].astype(f32)
    halves[...] = total.astype(half)
    for d in range(1, NZ):
        sender.start(
            halves.at[(z + d) % NZ],
            from_z.at[d - 1],
            recv_z.at[d - 1],
            at((z + d) % NZ, x, y, core),
        )

    for way in range(2):
        for group in range(2):
            region = halo_in.at[way, :, :, pl.ds(group * wide, wide)]
            landed(region, back_recv.at[way, group])
    for k, kept in enumerate((dk, dv)):
        low, high = pl.ds(0, HALO), pl.ds(rows - HALO, HALO)
        kept[low, :] = kept[low, :] + halo_in[1, k].astype(f32)
        kept[high, :] = kept[high, :] + halo_in[0, k].astype(f32)

    @pl.loop(0, width // 128)
    def _(p):
        columns = lane(p * 128, 128)
        grad, unit = dk[:, columns], k_unit[:, columns]
        gk[:, columns] = (
            k_factor[:, columns] * (grad - unit * head_mean(grad * unit))
        ).astype(half)
        gv[:, columns] = dv[:, columns].astype(half)

    @pl.loop(0, width // TILE)
    def _(t):
        columns = lane(t * TILE, TILE)
        blocks = wqkv.at[pl.ds(2 * t, 2)]
        keys = blocks[:, :, :, pl.ds(width, width)].reshape(TILE, width)
        held = blocks[:, :, :, pl.ds(2 * width, width)].reshape(TILE, width)
        gn[:, columns] = (
            gn[:, columns] + mat_back(gk[...], keys) + mat_back(gv[...], held)
        )

    @pl.loop(0, rows // 32)
    def _(t):
        block = pl.ds(pl.multiple_of(t * 32, 32), 32)
        grad, unit = gn[block, :], normal[block, :]
        centre = jnp.mean(grad, axis=1, keepdims=True)
        along = jnp.mean(grad * unit, axis=1, keepdims=True)
        change = factor[block, pl.ds(0, 1)] * (grad - centre - unit * along)
        out[block, :] = (gs[block, :].astype(f32) + change).astype(half)

    for d in range(1, NZ):
        landed(from_z.at[d - 1], recv_z.at[d - 1])
    total = halves[z].astype(f32)
    for d in range(1, NZ):
        total = total + from_z[d - 1].astype(f32)
    for k in range(pieces.shape[0]):
        pieces[k] = total[2 * k : 2 * k + 2, :]
    for dc in range(2):
        for dy in range(NY):
            if dy or dc:
                to_y, to_core = (y + dy) % NY, (core + dc) % 2
                index = (to_y % 4) * 4 + (to_y // 4) * 2 + to_core
                slot = dc * NY + dy
                sender.start(
                    pieces.at[index],
                    from_y.at[slot],
                    recv_y.at[slot],
                    at(z, x, to_y, to_core),
                )
    for dc in range(2):
        total = jnp.zeros(pieces.shape[1:], f32)
        for dy in range(NY):
            slot = dc * NY + dy
            if slot:
                landed(from_y.at[slot], recv_y.at[slot])
                total = total + from_y[slot]
            else:
                total = total + pieces[(y % 4) * 4 + (y // 4) * 2 + core]
        out_sum[:, (mine, other)[dc]] = total
    sender.finish()


def shards(
    nodes, w_query, w_key, w_value, w_output, w_head, neighbours, edge_counts, target, node_area
):
    rows, width = nodes.shape[2:]
    variables = w_head.shape[1]
    wide, block = width // 2, width // NZ // NX
    own = width // (NZ * NX * 2 * NY)
    f32, half = jnp.float32, jnp.bfloat16

    def vmem(shape, kind=half):
        return pltpu.VMEM(shape, kind)

    full = (rows, width)
    dma = pltpu.SemaphoreType.DMA
    scratch = [
        vmem((NZ, NX, block, 3 * width)),
        vmem((NZ, NX, block, width)),
        vmem((NZ, NX, block, variables)),
        vmem(full, f32),
        vmem(full),
        vmem((rows, 128), f32),
        vmem(full, f32),
        vmem(full, f32),
        vmem(full, f32),
        vmem(full, f32),
        vmem(full),
        vmem((2, EXT, width)),
        vmem((rows, EXT), f32),
        vmem((HEADS, rows, EXT), f32),
        vmem((2, rows, width)),
        vmem((2, rows, wide)),
        vmem(full),
        vmem((rows, variables), f32),
        vmem((4, rows, variables)),
        vmem(full),
        vmem(full),
        vmem(full),
        vmem(full, f32),
        vmem(full, f32),
        vmem(full),
        vmem(full),
        vmem(full, f32),
        vmem((2, 2, HALO, width)),
        vmem((2, 2, HALO, width)),
        vmem((NZ, NX, block, wide)),
        vmem((NX - 1, NZ, block, wide)),
        vmem((NZ, block, wide)),
        vmem((NZ - 1, block, wide)),
        vmem((2 * NY, own, wide), f32),
        vmem((2 * NY, own, wide), f32),
        dma((5,)),
        dma((160,)),
        dma((21,)),
        dma((17,)),
        dma((10,)),
        dma((3,)),
        dma((2, width // TILE)),
        dma((2, width // TILE)),
        dma((2, 2)),
        dma((3,)),
        dma((2,)),
        dma((NX - 1,)),
        dma((NZ - 1,)),
        dma((2 * NY,)),
    ]
    inside = pl.BlockSpec(memory_space=pltpu.VMEM)
    outside = pl.BlockSpec(memory_space=pl.ANY)
    grad_nodes, grad_out_proj = pl.pallas_call(
        layer_kernel,
        out_shape=[
            jax.ShapeDtypeStruct(full, half),
            jax.ShapeDtypeStruct((own, width), f32),
        ],
        in_specs=[inside] + [outside] * 5 + [inside] * 4,
        out_specs=[inside, inside],
        scratch_shapes=scratch,
        compiler_params=pltpu.CompilerParams(
            collective_id=0, has_side_effects=True, vmem_limit_bytes=48 * 2**20
        ),
        name="layer",
    )(
        nodes.reshape(full),
        w_query,
        w_key,
        w_value,
        w_output,
        w_head,
        neighbours,
        edge_counts.reshape(rows, 1),
        target.reshape(rows, variables),
        node_area.reshape(rows, 1),
    )
    return grad_nodes.reshape(nodes.shape), grad_out_proj.reshape(-1)


def solution(mesh):
    placed = (
        P("dp", "ens", "node", None),
        P("node", None),
        P("node", None),
        P("node", None),
        P("node", None),
        P("node", None),
        P("node", None),
        P("node"),
        P("dp", "node", None),
        P("node"),
    )
    return jax.shard_map(
        shards,
        mesh=mesh,
        in_specs=placed,
        out_specs=(P("dp", "ens", "node", None), P(("node", "ens", "dp"))),
        check_vma=False,
    )
```

time: 699 us -> 119 us (0.17)
  waiting for transfers between devices: 530 us -> 0 us
  Pallas kernels: 0 us -> 112 us
  blocking collectives: 60.5 us -> 0 us
  matrix products: 32.9 us -> 0 us
  local copies, waits for them, and re-layouts: 29.9 us -> 5.62 us
  starting transfers between devices: 14.8 us -> 0 us
  other arithmetic: 13.8 us -> 0 us
  between operations: 14.5 us -> 0.71 us
    unnamed x6 -> x0, waiting for transfers between devices: 264 us -> none
    all_gather x4 -> x0, waiting for transfers between devices: 260 us -> none  [the longest x1 80.9 us: shards(): lax.all_gather(w_value, 'node', axis=0, tiled=True)]
    pallas_call x0 -> x1, Pallas kernels: none -> 112 us  [shards(): pl.pallas_call(layer_kernel, out_shape=[jax.ShapeDtypeStruct(full, half),...]
    all_gather x2 -> x0, blocking collectives: 60.5 us -> none  [the longest x1 49.2 us: shards(): lax.all_gather(w_head, 'node', axis=0, tiled=True)]
    dot_general x34 -> x0, matrix products: 32.9 us -> none  [the longest x4 8.47 us: shards(): jnp.einsum('hij,ihd->jhd', attention_half, grad_group, preferred_element_...]
    ppermute x4 -> x0, starting transfers between devices: 14.6 us -> none  [the longest x2 8.77 us: passed_along(): return lax.ppermute(block, axis, route)]
    scatter-add x2 -> x0, local copies, waits for them, and re-layouts: 13.9 us -> none  [the longest x1 7.68 us: shards(): local_grad = local_grad.at[:reach_rows].add(from_lower)]
  transfers between devices with their start and end apart: 9 -> 0, of which waited for: 6 -> 0; matrix products, arithmetic and copies ran while one was open for 7% -> 0% of each run, Pallas kernels for 0% -> 0%
where the time goes in v1:
time: 119 us
  Pallas kernels  112 us (94%)
  local copies, waits for them, and re-layouts  5.62 us (5%)
    pallas_call x1, Pallas kernels, shards(): pl.pallas_call(layer_kernel, out_shape=[jax.ShapeDtypeStruct(full, half),...  112 us
    unnamed x21, local copies, waits for them, and re-layouts  5.4 us

profile of v1, /device:TPU:1, one launch (start us, length us, event | category | flops | bytes accessed | tf_op | source)
XLA Modules:
  0.0 118.7 jit_solution(13509578097781317245)
XLA Ops:
  0.6 0.0 copy-start.7
  0.6 0.0 copy-start.8
  0.7 0.0 copy-start.3
  0.7 0.0 copy-start.6
  0.7 0.8 copy.12.neighbours
  1.5 0.0 copy-done.7
  1.5 0.0 copy-start.1
  1.5 0.0 copy-start.2
  1.5 0.1 copy.13.counts
  1.6 0.0 copy-done.8
  1.7 0.1 copy.14.area
  1.8 0.0 copy-done.3
  1.8 0.0 copy-done.6
  1.8 0.6 copy-done.1
  2.4 0.0 copy-done.2
  2.4 0.0 copy-start
  2.4 0.9 copy-done
  3.3 0.0 copy-start.4
  3.3 0.8 copy-done.4
  4.2 0.0 copy-start.5
  4.2 0.8 copy-done.5
  5.0 112.3 %layer.1 = (bf16[128,1024]{1,0:T(8,128)(2,1)S(1)}, f32[2,1024]{1,0:T(2,128)S(1)}) custom-call(bf16[128,1024]{1,0:T(8,128)(2,1)S(1)} %bitcast.9, bf16[32,1024]{1,0:T(8,128)(2,1)S(1)} %copy-done.1, bf16[32,1024]{1,0:T(8,128)(2,1)S(1)} %copy-done.2, bf16[32,1024]{1,0:T(8,128)(2,1)S(1)} %copy-done.3, bf16[32,1024]{1,0:T(8,128)(2,1)S(1)} %copy-done.4, ...), custom_call_target="tpu_custom_call" | custom-call | tf_op jit(solution)/shard_map/layer/pallas_call | solution.py:671
  117.4 0.6 copy.17
  118.0 0.7 copy.19
Async XLA Ops:
  0.6 0.9 copy-start.7
  0.6 1.0 copy-start.8
  0.7 1.1 copy-start.3
  0.7 1.1 copy-start.6
  1.5 0.8 copy-start.1
  1.5 0.9 copy-start.2
  2.4 0.9 copy-start
  3.3 0.8 copy-start.4
  4.2 0.8 copy-start.5

commit v2 on v1

--- a/solution.py
+++ b/solution.py
@@ -27,8 +27,8 @@
 
 
 class Sender:
-    def __init__(self, sems):
-        self.sems, self.count, self.sent = sems, 0, []
+    def __init__(self, sems, first=0):
+        self.sems, self.count, self.sent = sems, first, []
 
     def start(self, src, dst, recv_sem, device):
         copy = pltpu.make_async_remote_copy(
@@ -63,7 +63,10 @@
 TILE = 256
 HALO = 32
 EXT = 256
-FIRST = 1024
+FIRST = 2048
+BY_X = 384
+SENDS = 130
+ORDER = (0, -1, 1, -2, 2, -3, 3, 4)
 
 
 def spread(z):
@@ -71,11 +74,11 @@
 
 
 class Gather:
-    def __init__(self, whole, sender, recv, pair):
-        self.whole, self.sender, self.recv, self.pair = whole, sender, recv, pair
-        self.z, self.x, self.y, self.core = place()
-        z, x, y, core = self.z, self.x, self.y, self.core
-        self.half = pl.ds(pl.multiple_of(core * 16, 16), 16)
+    def __init__(self, whole, rows, columns, sender, recv, pair):
+        self.whole, self.rows, self.columns = whole, rows, columns
+        self.sender, self.recv, self.pair = sender, recv, pair
+        z, x, y, core = place()
+        self.z, self.x, self.y, self.core = z, x, y, core
         self.near = [at(z, (x + d) % NX, y, core) for d in (1, 2, 3)]
         self.up = at((z + 1) % NZ, x, y, core)
         self.down = at((z + NZ - 1) % NZ, x, y, core)
@@ -84,102 +87,116 @@
     def send(self, region, sem, peer):
         self.sender.start(region, region, self.recv.at[sem], peer)
 
+    def landed(self, region, sem):
+        landed(region, self.recv.at[sem])
+
     def share(self, region):
         self.sender.start(region, region, self.pair, self.twin)
 
-    def paired(self):
-        landed(self.whole.at[:, :, pl.ds(0, 16)], self.pair)
-
-    def own(self, columns):
-        return self.whole.at[self.z, self.x, self.half, columns]
-
-    def line(self, dz, columns):
-        return self.whole.at[spread(self.z + dz), :, self.half, columns]
-
-    def one(self, dz, columns):
-        return self.whole.at[spread(self.z + dz), self.x, self.half, columns]
-
-    def across(self, columns, base):
+    def block(self, dz, dx, columns=None):
+        z, x = spread(self.z + dz), (self.x + dx + NX) % NX
+        return self.whole.at[z, x, self.rows, columns or self.columns]
+
+    def line(self, dz, columns=None):
+        return self.whole.at[
+            spread(self.z + dz), :, self.rows, columns or self.columns
+        ]
+
+
+    def across(self, base=0):
         for d in range(3):
-            self.send(self.own(columns), base + d, self.near[d])
-
-    def crossed(self, columns, base):
+            self.send(self.block(0, 0), base + d, self.near[d])
+
+    def crossed(self, base=0):
         for d in (1, 2, 3):
-            region = self.whole.at[
-                self.z, (self.x - d + NX) % NX, self.half, columns
-            ]
-            landed(region, self.recv.at[base + d - 1])
-
-    def pass_crossed(self, columns):
-        for d in (1, 2, 3):
-            self.share(
-                self.whole.at[self.z, (self.x - d + NX) % NX, self.half, columns]
-            )
-
-    def ring_begin(self, block, columns, base):
-        self.send(block(0, columns), base, self.up)
-        self.send(block(0, columns), base + 4, self.down)
-
-    def ring_step(self, block, columns, base, s, shared=True):
-        low, high = block(-s, columns), block(s, columns)
-        landed(low, self.recv.at[base + s - 1])
+            self.landed(self.block(0, -d), base + d - 1)
+
+    def ring_begin(self, columns, base):
+        self.send(self.line(0, columns), base, self.up)
+        self.send(self.line(0, columns), base + 4, self.down)
+
+    def ring_step(self, columns, base, s):
+        low, high = self.line(-s, columns), self.line(s, columns)
+        self.landed(low, base + s - 1)
         if s < 4:
             self.send(low, base + s, self.up)
-            landed(high, self.recv.at[base + s + 3])
+            self.landed(high, base + s + 3)
             if s < 3:
                 self.send(high, base + s + 4, self.down)
-        if shared:
-            self.share(low)
-            if s < 4:
-                self.share(high)
-
-    def column(self, dx, z0, count, columns):
-        x = (self.x + dx + NX) % NX
-        return self.whole.at[pl.ds(z0, count), x, self.half, columns]
-
-    def column_begin(self, columns, base):
-        region = self.column(0, 0, NZ, columns)
-        self.send(region, base, self.near[0])
-        self.send(region, base + 1, self.near[2])
-
-    def column_step(self, columns, base):
-        for sem, dx, z0, peer in (
-            (base, -1, 0, self.near[0]),
-            (base + 1, 1, 4, self.near[2]),
-        ):
-            region = self.column(dx, 0, NZ, columns)
-            landed(region, self.recv.at[sem])
-            self.send(self.column(dx, z0, 4, columns), sem + 2, peer)
+        self.share(low)
+        if s < 4:
+            self.share(high)
+
+
+    def fan(self, index):
+        region = self.block(ORDER[index], 0)
+        self.send(region, 7 + index, self.near[0])
+        self.send(region, 15 + index, self.near[2])
+
+    def column_begin(self):
+        self.send(self.block(0, 0), 0, self.up)
+        self.send(self.block(0, 0), 4, self.down)
+        self.fan(0)
+
+    def column_step(self, s):
+        low, high = self.block(-s, 0), self.block(s, 0)
+        self.landed(low, s - 1)
+        if s < 4:
+            self.send(low, s, self.up)
+        self.fan(ORDER.index(-s if s < 4 else 4))
+        if s < 4:
+            self.landed(high, s + 3)
+            if s < 3:
+                self.send(high, s + 4, self.down)
+            self.fan(ORDER.index(s))
+        self.share(low)
+        if s < 4:
+            self.share(high)
+
+    def column_pass(self, index):
+        for dx, base, onward in ((-1, 7, self.near[0]), (1, 15, self.near[2])):
+            region = self.block(ORDER[index], dx)
+            self.landed(region, base + index)
+            if (index % 2 == 0) == (dx < 0):
+                self.send(region, 23 + index, onward)
             self.share(region)
 
-    def column_end(self, columns, base):
-        for sem, z0 in ((base + 2, 0), (base + 3, 4)):
-            region = self.column(2, z0, 4, columns)
-            landed(region, self.recv.at[sem])
-            self.share(region)
+    def column_end(self, index):
+        region = self.block(ORDER[index], 2)
+        self.landed(region, 23 + index)
+        self.share(region)
+
+
+    def plane(self):
+        z, x, y, core = self.z, self.x, self.y, self.core
+        for d in range(1, NZ):
+            self.send(self.line(0), 2 + d, at((z + d) % NZ, x, y, core))
+
+    def planed(self):
+        for d in range(1, NZ):
+            self.landed(self.line(-d), 2 + d)
+
 
     def slab(self, dy):
         width = self.whole.shape[3] // NY
         first = pl.multiple_of(((self.y + dy + NY) % NY) * width, width)
-        return self.whole.at[:, :, self.half, pl.ds(first, width)]
-
-    def y_begin(self, base):
+        return self.whole.at[:, :, self.rows, pl.ds(first, width)]
+
+    def y_begin(self, base=10):
+        z, x, y, core = self.z, self.x, self.y, self.core
+        self.send(self.slab(0), base, at(z, x, (y + 1) % NY, core))
+        self.send(self.slab(0), base + 4, at(z, x, (y + NY - 1) % NY, core))
         self.share(self.slab(0))
-        y, core = self.y, self.core
-        self.send(self.slab(0), base, at(self.z, self.x, (y + 1) % NY, core))
-        self.send(self.slab(0), base + 4, at(self.z, self.x, (y + NY - 1) % NY, core))
-
-    def y_step(self, base, s):
-        y, core = self.y, self.core
+
+    def y_step(self, s, base=10):
+        z, x, y, core = self.z, self.x, self.y, self.core
         low, high = self.slab(-s), self.slab(s)
-        landed(low, self.recv.at[base + s - 1])
+        self.landed(low, base + s - 1)
         if s < 4:
-            self.send(low, base + s, at(self.z, self.x, (y + 1) % NY, core))
-            landed(high, self.recv.at[base + s + 3])
+            self.send(low, base + s, at(z, x, (y + 1) % NY, core))
+            self.landed(high, base + s + 3)
             if s < 3:
-                self.send(
-                    high, base + s + 4, at(self.z, self.x, (y + NY - 1) % NY, core)
-                )
+                self.send(high, base + s + 4, at(z, x, (y + NY - 1) % NY, core))
         self.share(low)
         if s < 4:
             self.share(high)
@@ -241,107 +258,170 @@
 
 
 def layer_kernel(
-    nodes, wq_shard, wk_shard, wv_shard, wo_shard, wh_shard, neighbours, counts,
-    target, area, out, out_sum,
+    nodes_in, wq_shard, wk_shard, wv_shard, wo_shard, wh_shard, neighbours_in,
+    counts_in, target_in, area_in, out, out_sum,
+    nodes, neighbours, counts, target, area,
     wqkv, wo, wh, normal, normed, factor, q_unit, k_unit, q_factor, k_factor, q_half,
     kv, near, attention, left, right, settled, differ, differs, gs, gm, gq, dk, dv,
-    gk, gv, gn, halo_out, halo_in, parts, from_x, halves, from_z, pieces, from_y,
+    gk, gv, gn, halo_out, halo_in, parts, from_x, halves, from_z, parts_b, from_z_b,
+    halves_b, from_x_b, pieces, from_y,
     local, send, recv_a, recv_o, recv_h, pair, halo_send, halo_recv, back_recv,
-    ens_recv, recv_core, recv_x, recv_z, recv_y,
+    ens_recv, recv_core, recv_x, recv_z, recv_x_b, recv_z_b, recv_y,
 ):
     f32, half = jnp.float32, jnp.bfloat16
     z, x, y, core = place()
     node = z * NX + x
     rows, width = nodes.shape
-    sender = Sender(send)
+    small = [
+        pltpu.make_async_copy(source, kept, local.at[k])
+        for k, (source, kept) in enumerate(
+            (
+                (nodes_in, nodes),
+                (neighbours_in, neighbours),
+                (counts_in, counts),
+                (target_in, target),
+                (area_in, area),
+            )
+        )
+    ]
     own_half = pl.ds(pl.multiple_of(core * 16, 16), 16)
-    loads = []
     slab = pl.ds(pl.multiple_of(y * 128, 128), 128)
-    all_columns = pl.ds(0, width)
+    every = pl.ds(0, width)
     every_h = pl.ds(0, wh_shard.shape[1])
-    for k, (shard, whole, taken, kept) in enumerate(
-        (
-            (wq_shard, wqkv, all_columns, pl.ds(0, width)),
-            (wk_shard, wqkv, all_columns, pl.ds(width, width)),
-            (wv_shard, wqkv, all_columns, pl.ds(2 * width, width)),
-            (wo_shard, wo, slab, slab),
-            (wh_shard, wh, every_h, every_h),
-        )
-    ):
-        load = pltpu.make_async_copy(
-            shard.at[own_half, taken],
-            whole.at[z, x, own_half, kept],
-            local.at[k],
-        )
+
+    def own(k, shard, whole, taken_rows, taken, kept):
+        return pltpu.make_async_copy(
+            shard.at[taken_rows, taken],
+            whole.at[z, x, taken_rows, kept],
+            local.at[5 + k],
+        )
+
+    all_rows = pl.ds(0, wq_shard.shape[0])
+    own_o = own(0, wo_shard, wo, own_half, slab, slab)
+    own_h = own(1, wh_shard, wh, own_half, every_h, every_h)
+
+    def own_a(which):
+        if which:
+            kept = pl.ds(FIRST, width)
+            return [own(2, wv_shard, wqkv, all_rows, every, kept)]
+        return [
+            own(2, wq_shard, wqkv, all_rows, every, pl.ds(0, width)),
+            own(3, wk_shard, wqkv, all_rows, every, pl.ds(width, width)),
+        ]
+
+    def normalise():
+        small[0].wait()
+        values = nodes[...].astype(f32)
+        shifted = values - jnp.mean(values, axis=1, keepdims=True)
+        scale = lax.rsqrt(jnp.mean(shifted * shifted, axis=1, keepdims=True) + 1e-05)
+        factor[...] = jnp.broadcast_to(scale, factor.shape)
+        normal[...] = shifted * scale
+        normed[...] = normal[...].astype(half)
+
+    def find_near():
+        small[1].wait()
+        small[2].wait()
+        total = NZ * NX * rows
+        column = (neighbours[...] - node * rows + HALO + total) & (total - 1)
+        at_column = lax.broadcasted_iota(jnp.int32, (EXT, rows), 0)
+        hits = jnp.zeros((EXT, rows), f32)
+        for s in range(neighbours.shape[0]):
+            hit = (column[s : s + 1, :] == at_column) & (counts[...] > s)
+            hits = hits + jnp.where(hit, 1.0, 0.0)
+        near[...] = hits.T
+        kv[:, pl.ds(rows + 2 * HALO, EXT - rows - 2 * HALO)] = jnp.zeros(
+            (2, EXT - rows - 2 * HALO, width), half
+        )
+
+    def gather(which):
+        sender = Sender(send)
+        columns = (pl.ds(0, FIRST), pl.ds(FIRST, 3 * width - FIRST))
+        ga = Gather(wqkv, all_rows, columns[which], sender, recv_a, pair.at[0])
+        go = Gather(wo, own_half, slab, sender, recv_o, pair.at[1])
+        gh = Gather(wh, own_half, every_h, sender, recv_h, pair.at[2])
+        for load in own_a(which):
+            load.wait()
+        if which:
+            ga.across()
+        else:
+            ga.column_begin()
+        own_o.wait()
+        go.across()
+        own_h.wait()
+        gh.across()
+        ga.share(ga.block(0, 0))
+        normalise()
+        if which:
+            chunk = (3 * width - FIRST) // 2
+            chunks = [(pl.ds(FIRST + k * chunk, chunk), 3 + 7 * k) for k in range(2)]
+            ga.crossed()
+            for part in chunks:
+                ga.ring_begin(*part)
+            go.crossed()
+            go.plane()
+            for d in (1, 2, 3):
+                ga.share(ga.block(0, -d))
+            find_near()
+            for s in (1, 2, 3, 4):
+                for part in chunks:
+                    ga.ring_step(*part, s)
+                if s == 1:
+                    go.planed()
+                    go.y_begin()
+                if s == 3:
+                    go.y_step(1)
+                    gh.crossed()
+                    gh.plane()
+            go.y_step(2)
+        else:
+            ga.column_step(1)
+            go.crossed()
+            go.plane()
+            ga.column_pass(0)
+            ga.column_step(2)
+            find_near()
+            ga.column_pass(1)
+            go.planed()
+            go.y_begin()
+            ga.column_step(3)
+            ga.column_pass(2)
+            ga.column_step(4)
+            ga.column_pass(3)
+            gh.crossed()
+            gh.plane()
+            ga.column_pass(4)
+            ga.column_end(0)
+            go.y_step(1)
+            ga.column_pass(5)
+            ga.column_end(1)
+            ga.column_pass(6)
+            ga.column_end(2)
+            ga.column_pass(7)
+            for index in (3, 4, 5, 6, 7):
+                ga.column_end(index)
+            go.y_step(2)
+        landed(wqkv.at[:, :, :, columns[1 - which]], pair.at[0])
+        sender.finish()
+
+    for which in range(2):
+        @pl.when(core == which)
+        def _():
+            for load in own_a(which):
+                load.start()
+
+    own_o.start()
+    own_h.start()
+    for load in small:
         load.start()
-        loads.append(load)
     greet(all_peers())
-    for load in loads:
-        load.wait()
-
-    ga = Gather(wqkv, sender, recv_a, pair.at[0])
-    go = Gather(wo, sender, recv_o, pair.at[1])
-    gh = Gather(wh, sender, recv_h, pair.at[2])
-    first, last = pl.ds(0, FIRST), pl.ds(FIRST, 3 * width - FIRST)
-    ga.across(last, 0)
-    ga.ring_begin(ga.one, first, 3)
-    go.across(slab, 0)
-    gh.across(every_h, 0)
-    ga.share(ga.own(pl.ds(0, 3 * width)))
-    gh.share(gh.own(every_h))
-
-    values = nodes[...].astype(f32)
-    shifted = values - jnp.mean(values, axis=1, keepdims=True)
-    scale = lax.rsqrt(jnp.mean(shifted * shifted, axis=1, keepdims=True) + 1e-05)
-    factor[...] = jnp.broadcast_to(scale, factor.shape)
-    normal[...] = shifted * scale
-    normed[...] = normal[...].astype(half)
-
-    ga.crossed(last, 0)
-    ga.ring_begin(ga.line, last, 10)
-    ga.ring_step(ga.one, first, 3, 1)
-    go.crossed(slab, 0)
-    go.ring_begin(go.line, slab, 3)
-    gh.crossed(every_h, 0)
-    gh.ring_begin(gh.line, every_h, 3)
-    ga.pass_crossed(last)
-    gh.pass_crossed(every_h)
-
-    column = (
-        neighbours[...] - node * rows + HALO + NZ * NX * rows
-    ) & (NZ * NX * rows - 1)
-    at_column = lax.broadcasted_iota(jnp.int32, (rows, EXT), 1)
-    hits = jnp.zeros((rows, EXT), f32)
-    for s in range(neighbours.shape[1]):
-        hit = (column[:, s : s + 1] == at_column) & (counts[...] > s)
-        hits = hits + jnp.where(hit, 1.0, 0.0)
-    near[...] = hits
-    kv[:, pl.ds(rows + 2 * HALO, EXT - rows - 2 * HALO)] = jnp.zeros(
-        (2, EXT - rows - 2 * HALO, width), half
-    )
-
-    ga.ring_step(ga.one, first, 3, 2)
-    go.ring_step(go.line, slab, 3, 1, False)
-    ga.ring_step(ga.one, first, 3, 3)
-    go.ring_step(go.line, slab, 3, 2, False)
-    gh.ring_step(gh.line, every_h, 3, 1)
-    ga.ring_step(ga.one, first, 3, 4)
-    ga.column_begin(first, 17)
-    go.ring_step(go.line, slab, 3, 3, False)
-    ga.ring_step(ga.line, last, 10, 1)
-    gh.ring_step(gh.line, every_h, 3, 2)
-    go.ring_step(go.line, slab, 3, 4, False)
-    go.y_begin(10)
-    ga.ring_step(ga.line, last, 10, 2)
-    gh.ring_step(gh.line, every_h, 3, 3)
-    go.y_step(10, 1)
-    ga.column_step(first, 17)
-    ga.ring_step(ga.line, last, 10, 3)
-    gh.ring_step(gh.line, every_h, 3, 4)
-    go.y_step(10, 2)
-    ga.column_end(first, 17)
-    ga.ring_step(ga.line, last, 10, 4)
-    ga.paired()
+    for which in range(2):
+        @pl.when(core == which)
+        def _():
+            gather(which)
+
+    sender = Sender(send, SENDS)
+    go = Gather(wo, own_half, slab, sender, recv_o, pair.at[1])
+    gh = Gather(wh, own_half, every_h, sender, recv_h, pair.at[2])
 
     before, after = (
         {"node": (node + NZ * NX - 1) % (NZ * NX)},
@@ -386,7 +466,9 @@
         halo(t, 0).start()
         halo(t, 1).start()
 
-    go.y_step(10, 3)
+    go.y_step(3)
+    gh.planed()
+    gh.share(wh.at[:, :, own_half])
 
     @pl.loop(0, width // TILE)
     def _(t):
@@ -407,9 +489,11 @@
 
     twin = at(z, x, y, 1 - core)
     sender.start(left.at[0], left.at[1], recv_core.at[0], twin)
-    go.y_step(10, 4)
-    go.paired()
-    gh.paired()
+    go.y_step(4)
+    landed(wo.at[:, :, pl.ds(0, 16)], pair.at[1])
+    landed(wh.at[:, :, pl.ds(0, 16)], pair.at[2])
+    small[3].wait()
+    small[4].wait()
 
     @pl.loop(0, width // TILE)
     def _(t):
@@ -434,7 +518,8 @@
         2 * members * members
     )
     core_grad = own_sign / members - 2 * coefficient * paired
-    grad_pred = (area[...] * core_grad).astype(half)
+    weight = jnp.broadcast_to(area[...], (rows, rows)).T
+    grad_pred = (weight * core_grad).astype(half)
 
     @pl.loop(0, width // TILE)
     def _(t):
@@ -460,7 +545,8 @@
         columns = lane(block * tall, tall)
         total = mat_across(left[0, :, columns], right[0])
         total = total + mat_across(left[1, :, columns], right[1])
-        parts[block] = total.astype(half).reshape(parts.shape[1:])
+        parts[block] = total[:, :BY_X].astype(half).reshape(parts.shape[1:])
+        parts_b[block] = total[:, BY_X:].astype(half).reshape(parts_b.shape[1:])
 
     for d in range(1, NX):
         sender.start(
@@ -468,6 +554,13 @@
             from_x.at[d - 1],
             recv_x.at[d - 1],
             at(z, (x + d) % NX, y, core),
+        )
+    for d in range(1, NZ):
+        sender.start(
+            parts_b.at[(z + d) % NZ],
+            from_z_b.at[d - 1],
+            recv_z_b.at[d - 1],
+            at((z + d) % NZ, x, y, core),
         )
 
     for group in range(2):
@@ -531,6 +624,19 @@
             recv_z.at[d - 1],
             at((z + d) % NZ, x, y, core),
         )
+    for d in range(1, NZ):
+        landed(from_z_b.at[d - 1], recv_z_b.at[d - 1])
+    total = parts_b[z].astype(f32)
+    for d in range(1, NZ):
+        total = total + from_z_b[d - 1].astype(f32)
+    halves_b[...] = total.astype(half)
+    for d in range(1, NX):
+        sender.start(
+            halves_b.at[(x + d) % NX],
+            from_x_b.at[d - 1],
+            recv_x_b.at[d - 1],
+            at(z, (x + d) % NX, y, core),
+        )
 
     for way in range(2):
         for group in range(2):
@@ -574,8 +680,14 @@
     total = halves[z].astype(f32)
     for d in range(1, NZ):
         total = total + from_z[d - 1].astype(f32)
+    for d in range(1, NX):
+        landed(from_x_b.at[d - 1], recv_x_b.at[d - 1])
+    total_b = halves_b[x].astype(f32)
+    for d in range(1, NX):
+        total_b = total_b + from_x_b[d - 1].astype(f32)
     for k in range(pieces.shape[0]):
-        pieces[k] = total[2 * k : 2 * k + 2, :]
+        pieces[k, :, :BY_X] = total[2 * k : 2 * k + 2, :]
+        pieces[k, :, BY_X:] = total_b[2 * k : 2 * k + 2, :]
     for dc in range(2):
         for dy in range(NY):
             if dy or dc:
@@ -597,7 +709,11 @@
                 total = total + from_y[slot]
             else:
                 total = total + pieces[(y % 4) * 4 + (y // 4) * 2 + core]
-        out_sum[:, (mine, other)[dc]] = total
+        per = wide // 128
+        for i in range(total.shape[0]):
+            for j in range(per):
+                first = i * NY + (core + dc) % 2 * per + j
+                out_sum[pl.ds(first, 1), :] = total[i : i + 1, j * 128 : j * 128 + 128]
     sender.finish()
 
 
@@ -616,6 +732,11 @@
     full = (rows, width)
     dma = pltpu.SemaphoreType.DMA
     scratch = [
+        vmem(full),
+        vmem((neighbours.shape[1], rows), jnp.int32),
+        vmem((1, rows), jnp.int32),
+        vmem((rows, variables), f32),
+        vmem((1, rows), f32),
         vmem((NZ, NX, block, 3 * width)),
         vmem((NZ, NX, block, width)),
         vmem((NZ, NX, block, variables)),
@@ -645,15 +766,19 @@
         vmem(full, f32),
         vmem((2, 2, HALO, width)),
         vmem((2, 2, HALO, width)),
-        vmem((NZ, NX, block, wide)),
-        vmem((NX - 1, NZ, block, wide)),
-        vmem((NZ, block, wide)),
-        vmem((NZ - 1, block, wide)),
+        vmem((NZ, NX, block, BY_X)),
+        vmem((NX - 1, NZ, block, BY_X)),
+        vmem((NZ, block, BY_X)),
+        vmem((NZ - 1, block, BY_X)),
+        vmem((NZ, NX, block, wide - BY_X)),
+        vmem((NZ - 1, NX, block, wide - BY_X)),
+        vmem((NX, block, wide - BY_X)),
+        vmem((NX - 1, block, wide - BY_X)),
         vmem((2 * NY, own, wide), f32),
         vmem((2 * NY, own, wide), f32),
-        dma((5,)),
-        dma((160,)),
-        dma((21,)),
+        dma((9,)),
+        dma((SENDS + 64,)),
+        dma((31,)),
         dma((17,)),
         dma((10,)),
         dma((3,)),
@@ -664,21 +789,23 @@
         dma((2,)),
         dma((NX - 1,)),
         dma((NZ - 1,)),
+        dma((NX - 1,)),
+        dma((NZ - 1,)),
         dma((2 * NY,)),
     ]
     inside = pl.BlockSpec(memory_space=pltpu.VMEM)
-    outside = pl.BlockSpec(memory_space=pl.ANY)
+    outside = pl.BlockSpec(memory_space=pltpu.HBM)
     grad_nodes, grad_out_proj = pl.pallas_call(
         layer_kernel,
         out_shape=[
             jax.ShapeDtypeStruct(full, half),
-            jax.ShapeDtypeStruct((own, width), f32),
+            jax.ShapeDtypeStruct((own * NY, width // NY), f32),
         ],
-        in_specs=[inside] + [outside] * 5 + [inside] * 4,
+        in_specs=[outside] * 10,
         out_specs=[inside, inside],
         scratch_shapes=scratch,
         compiler_params=pltpu.CompilerParams(
-            collective_id=0, has_side_effects=True, vmem_limit_bytes=48 * 2**20
+            collective_id=0, has_side_effects=True, vmem_limit_bytes=62 * 2**20
         ),
         name="layer",
     )(
@@ -688,10 +815,10 @@
         w_value,
         w_output,
         w_head,
-        neighbours,
-        edge_counts.reshape(rows, 1),
+        neighbours.T,
+        edge_counts.reshape(1, rows),
         target.reshape(rows, variables),
-        node_area.reshape(rows, 1),
+        node_area.reshape(1, rows),
     )
     return grad_nodes.reshape(nodes.shape), grad_out_proj.reshape(-1)
 

time: 119 us -> 100 us (0.84)
  Pallas kernels: 112 us -> 97.3 us
  local copies, waits for them, and re-layouts: 5.62 us -> 2.28 us
    pallas_call x1, Pallas kernels: 112 us -> 97.3 us  [shards(): pl.pallas_call(layer_kernel, out_shape=[jax.ShapeDtypeStruct(full, half),...]
    unnamed x21 -> x4, local copies, waits for them, and re-layouts: 5.4 us -> 2.28 us
where the time goes in v2:
time: 100 us
  Pallas kernels  97.3 us (97%)
  local copies, waits for them, and re-layouts  2.28 us (2%)
    pallas_call x1, Pallas kernels, shards(): pl.pallas_call(layer_kernel, out_shape=[jax.ShapeDtypeStruct(full, half),...  97.3 us
    unnamed x4, local copies, waits for them, and re-layouts  2.28 us

profile of v2, /device:TPU:1, one launch (start us, length us, event | category | flops | bytes accessed | tf_op | source)
XLA Modules:
  0.0 100.2 jit_solution(2430196023141588344)
XLA Ops:
  0.6 97.3 %layer.1 = (bf16[128,1024]{1,0:T(8,128)(2,1)}, f32[16,128]{1,0:T(8,128)}) custom-call(bf16[128,1024]{1,0:T(8,128)(2,1)} %bitcast.7, bf16[32,1024]{1,0:T(8,128)(2,1)} %wq_shard.1, bf16[32,1024]{1,0:T(8,128)(2,1)} %wk_shard.1, bf16[32,1024]{1,0:T(8,128)(2,1)} %wv_shard.1, bf16[32,1024]{1,0:T(8,128)(2,1)} %wo_shard.1, bf16[32,128]{1,0:T(8,128)(2,1)} %wh_shard.1, ...), custom_call_target="tpu_custom_call" | custom-call | tf_op jit(solution)/shard_map/layer/pallas_call | solution.py:798
  98.0 0.0 copy-start
  98.0 1.7 %copy.14 = bf16[1,1,128,1024]{3,2,1,0:T(8,128)(2,1)} copy(bf16[1,1,128,1024]{3,2,1,0:T(8,128)(2,1)} %bitcast.8) | data formatting | bytes 524288
  99.6 0.0 copy-done
  99.6 0.6 copy.15
Async XLA Ops:
  98.0 1.7 %copy-start = (f32[16,128]{1,0:T(8,128)S(1)}, f32[16,128]{1,0:T(8,128)}, u32[]{:S(2)}) copy-start(f32[16,128]{1,0:T(8,128)} %get-tuple-element.5) | copy-start | bytes 24580

commit v3 on v2

--- a/solution.py
+++ b/solution.py
@@ -63,7 +63,7 @@
 TILE = 256
 HALO = 32
 EXT = 256
-FIRST = 2048
+FIRST = 1792
 BY_X = 384
 SENDS = 130
 ORDER = (0, -1, 1, -2, 2, -3, 3, 4)
@@ -266,7 +266,7 @@
     gk, gv, gn, halo_out, halo_in, parts, from_x, halves, from_z, parts_b, from_z_b,
     halves_b, from_x_b, pieces, from_y,
     local, send, recv_a, recv_o, recv_h, pair, halo_send, halo_recv, back_recv,
-    ens_recv, recv_core, recv_x, recv_z, recv_x_b, recv_z_b, recv_y,
+    ens_recv, recv_core, send_x, recv_x, recv_z, recv_x_b, recv_z_b, recv_y,
 ):
     f32, half = jnp.float32, jnp.bfloat16
     z, x, y, core = place()
@@ -301,12 +301,17 @@
     own_h = own(1, wh_shard, wh, own_half, every_h, every_h)
 
     def own_a(which):
+        rest = FIRST - width
         if which:
-            kept = pl.ds(FIRST, width)
-            return [own(2, wv_shard, wqkv, all_rows, every, kept)]
+            end, kept = pl.ds(rest, width - rest), pl.ds(FIRST, width - rest)
+            loads = [own(2, wv_shard, wqkv, all_rows, every, pl.ds(2 * width, width))]
+            if rest < width:
+                loads.append(own(3, wk_shard, wqkv, all_rows, end, kept))
+            return loads
+        start = pl.ds(0, rest)
         return [
             own(2, wq_shard, wqkv, all_rows, every, pl.ds(0, width)),
-            own(3, wk_shard, wqkv, all_rows, every, pl.ds(width, width)),
+            own(3, wk_shard, wqkv, all_rows, start, pl.ds(width, rest)),
         ]
 
     def normalise():
@@ -372,7 +377,6 @@
                     go.y_step(1)
                     gh.crossed()
                     gh.plane()
-            go.y_step(2)
         else:
             ga.column_step(1)
             go.crossed()
@@ -399,7 +403,6 @@
             ga.column_pass(7)
             for index in (3, 4, 5, 6, 7):
                 ga.column_end(index)
-            go.y_step(2)
         landed(wqkv.at[:, :, :, columns[1 - which]], pair.at[0])
         sender.finish()
 
@@ -466,7 +469,7 @@
         halo(t, 0).start()
         halo(t, 1).start()
 
-    go.y_step(3)
+    go.y_step(2)
     gh.planed()
     gh.share(wh.at[:, :, own_half])
 
@@ -475,8 +478,7 @@
         halo(t, 0).wait()
         halo(t, 1).wait()
 
-    @pl.loop(0, width // 128)
-    def _(p):
+    def attend(p):
         columns = lane(p * 128, 128)
         keys, held = kv[0, :, columns], kv[1, :, columns]
         mixed = []
@@ -486,6 +488,11 @@
             attention[2 * p + side] = weight
             mixed.append(mat(weight.astype(half), held))
         left[0, :, columns] = jnp.where(head_side(), mixed[0], mixed[1]).astype(half)
+
+    pairs = width // 128
+    pl.loop(0, pairs // 2, unroll=2)(attend)
+    go.y_step(3)
+    pl.loop(pairs // 2, pairs, unroll=2)(attend)
 
     twin = at(z, x, y, 1 - core)
     sender.start(left.at[0], left.at[1], recv_core.at[0], twin)
@@ -540,6 +547,16 @@
     landed(right.at[1], recv_core.at[1])
     tall = width // NZ
 
+    def by_x(block, d):
+        return pltpu.make_async_remote_copy(
+            src_ref=parts.at[block, (x + d) % NX],
+            dst_ref=from_x.at[d - 1, block],
+            send_sem=send_x.at[d - 1, block],
+            recv_sem=recv_x.at[d - 1, block],
+            device_id=at(z, (x + d) % NX, y, core),
+            device_id_type=MESH,
+        )
+
     @pl.loop(0, NZ)
     def _(block):
         columns = lane(block * tall, tall)
@@ -547,14 +564,9 @@
         total = total + mat_across(left[1, :, columns], right[1])
         parts[block] = total[:, :BY_X].astype(half).reshape(parts.shape[1:])
         parts_b[block] = total[:, BY_X:].astype(half).reshape(parts_b.shape[1:])
-
-    for d in range(1, NX):
-        sender.start(
-            parts.at[:, (x + d) % NX],
-            from_x.at[d - 1],
-            recv_x.at[d - 1],
-            at(z, (x + d) % NX, y, core),
-        )
+        for d in range(1, NX):
+            by_x(block, d).start()
+
     for d in range(1, NZ):
         sender.start(
             parts_b.at[(z + d) % NZ],
@@ -611,8 +623,11 @@
         block = wqkv[pl.ds(2 * t, 2), :, :, pl.ds(0, width)].reshape(TILE, width)
         gn[:, lane(t * TILE, TILE)] = mat_back(gq[...], block)
 
-    for d in range(1, NX):
-        landed(from_x.at[d - 1], recv_x.at[d - 1])
+    @pl.loop(0, NZ)
+    def _(block):
+        for d in range(1, NX):
+            by_x(block, d).wait()
+
     total = parts[:, x].astype(f32)
     for d in range(1, NX):
         total = total + from_x[d - 1].astype(f32)
@@ -787,7 +802,8 @@
         dma((2, 2)),
         dma((3,)),
         dma((2,)),
-        dma((NX - 1,)),
+        dma((NX - 1, NZ)),
+        dma((NX - 1, NZ)),
         dma((NZ - 1,)),
         dma((NX - 1,)),
         dma((NZ - 1,)),

time: 100 us -> 97.8 us (0.978)
  Pallas kernels: 97.3 us -> 94.8 us
    pallas_call x1, Pallas kernels: 97.3 us -> 94.8 us  [shards(): pl.pallas_call(layer_kernel, out_shape=[jax.ShapeDtypeStruct(full, half),...]
where the time goes in v3:
time: 97.8 us; the launch traced here: 97.7 us
  Pallas kernels  94.8 us (97%)
  local copies, waits for them, and re-layouts  2.28 us (2%)
    pallas_call x1, Pallas kernels, shards(): pl.pallas_call(layer_kernel, out_shape=[jax.ShapeDtypeStruct(full, half),...  94.8 us
    unnamed x4, local copies, waits for them, and re-layouts  2.28 us

profile of v3, /device:TPU:1, one launch (start us, length us, event | category | flops | bytes accessed | tf_op | source)
XLA Modules:
  0.0 97.7 jit_solution(7644701808186740102)
XLA Ops:
  0.6 94.8 %layer.1 = (bf16[128,1024]{1,0:T(8,128)(2,1)}, f32[16,128]{1,0:T(8,128)}) custom-call(bf16[128,1024]{1,0:T(8,128)(2,1)} %bitcast.7, bf16[32,1024]{1,0:T(8,128)(2,1)} %wq_shard.1, bf16[32,1024]{1,0:T(8,128)(2,1)} %wk_shard.1, bf16[32,1024]{1,0:T(8,128)(2,1)} %wv_shard.1, bf16[32,1024]{1,0:T(8,128)(2,1)} %wo_shard.1, bf16[32,128]{1,0:T(8,128)(2,1)} %wh_shard.1, ...), custom_call_target="tpu_custom_call" | custom-call | tf_op jit(solution)/shard_map/layer/pallas_call | solution.py:814
  95.4 0.0 copy-start
  95.4 1.7 %copy.14 = bf16[1,1,128,1024]{3,2,1,0:T(8,128)(2,1)} copy(bf16[1,1,128,1024]{3,2,1,0:T(8,128)(2,1)} %bitcast.8) | data formatting | bytes 524288
  97.1 0.0 copy-done
  97.1 0.6 copy.15
Async XLA Ops:
  95.4 1.7 %copy-start = (f32[16,128]{1,0:T(8,128)S(1)}, f32[16,128]{1,0:T(8,128)}, u32[]{:S(2)}) copy-start(f32[16,128]{1,0:T(8,128)} %get-tuple-element.5) | copy-start | bytes 24580

commit v4 on v3

--- a/solution.py
+++ b/solution.py
@@ -65,6 +65,7 @@
 EXT = 256
 FIRST = 1792
 BY_X = 384
+STRAIGHT = (6, 7)
 SENDS = 130
 ORDER = (0, -1, 1, -2, 2, -3, 3, 4)
 
@@ -132,6 +133,8 @@
         region = self.block(ORDER[index], 0)
         self.send(region, 7 + index, self.near[0])
         self.send(region, 15 + index, self.near[2])
+        if index in STRAIGHT:
+            self.send(region, 23 + index, self.near[1])
 
     def column_begin(self):
         self.send(self.block(0, 0), 0, self.up)
@@ -157,7 +160,7 @@
         for dx, base, onward in ((-1, 7, self.near[0]), (1, 15, self.near[2])):
             region = self.block(ORDER[index], dx)
             self.landed(region, base + index)
-            if (index % 2 == 0) == (dx < 0):
+            if index not in STRAIGHT and (index % 2 == 0) == (dx < 0):
                 self.send(region, 23 + index, onward)
             self.share(region)
 
@@ -576,7 +579,7 @@
         )
 
     for group in range(2):
-        @pl.loop(group * 4, group * 4 + 4)
+        @pl.loop(group * 4, group * 4 + 4, unroll=2)
         def _(p):
             columns = lane(p * 128, 128)
             keys, held = kv[0, :, columns], kv[1, :, columns]
@@ -618,11 +621,6 @@
                 peer,
             )
 
-    @pl.loop(0, width // TILE)
-    def _(t):
-        block = wqkv[pl.ds(2 * t, 2), :, :, pl.ds(0, width)].reshape(TILE, width)
-        gn[:, lane(t * TILE, TILE)] = mat_back(gq[...], block)
-
     @pl.loop(0, NZ)
     def _(block):
         for d in range(1, NX):
@@ -639,6 +637,11 @@
             recv_z.at[d - 1],
             at((z + d) % NZ, x, y, core),
         )
+    @pl.loop(0, width // TILE)
+    def _(t):
+        block = wqkv[pl.ds(2 * t, 2), :, :, pl.ds(0, width)].reshape(TILE, width)
+        gn[:, lane(t * TILE, TILE)] = mat_back(gq[...], block)
+
     for d in range(1, NZ):
         landed(from_z_b.at[d - 1], recv_z_b.at[d - 1])
     total = parts_b[z].astype(f32)

time: 97.8 us -> 97.3 us (level)
  no operation moved by 1% of the time
where the time goes in v4:
time: 97.3 us; the launch traced here: 97.1 us
  Pallas kernels  94.2 us (97%)
  local copies, waits for them, and re-layouts  2.28 us (2%)
    pallas_call x1, Pallas kernels, shards(): pl.pallas_call(layer_kernel, out_shape=[jax.ShapeDtypeStruct(full, half),...  94.2 us
    unnamed x4, local copies, waits for them, and re-layouts  2.28 us

profile of v4, /device:TPU:1, one launch (start us, length us, event | category | flops | bytes accessed | tf_op | source)
XLA Modules:
  0.0 97.1 jit_solution(14210094483962258740)
XLA Ops:
  0.6 94.2 %layer.1 = (bf16[128,1024]{1,0:T(8,128)(2,1)}, f32[16,128]{1,0:T(8,128)}) custom-call(bf16[128,1024]{1,0:T(8,128)(2,1)} %bitcast.7, bf16[32,1024]{1,0:T(8,128)(2,1)} %wq_shard.1, bf16[32,1024]{1,0:T(8,128)(2,1)} %wk_shard.1, bf16[32,1024]{1,0:T(8,128)(2,1)} %wv_shard.1, bf16[32,1024]{1,0:T(8,128)(2,1)} %wo_shard.1, bf16[32,128]{1,0:T(8,128)(2,1)} %wh_shard.1, ...), custom_call_target="tpu_custom_call" | custom-call | tf_op jit(solution)/shard_map/layer/pallas_call | solution.py:817
  94.9 0.0 copy-start
  94.9 1.7 %copy.14 = bf16[1,1,128,1024]{3,2,1,0:T(8,128)(2,1)} copy(bf16[1,1,128,1024]{3,2,1,0:T(8,128)(2,1)} %bitcast.8) | data formatting | bytes 524288
  96.5 0.0 copy-done
  96.5 0.6 copy.15
Async XLA Ops:
  94.9 1.7 %copy-start = (f32[16,128]{1,0:T(8,128)S(1)}, f32[16,128]{1,0:T(8,128)}, u32[]{:S(2)}) copy-start(f32[16,128]{1,0:T(8,128)} %get-tuple-element.5) | copy-start | bytes 24580

commit v5 on v4

--- a/solution.py
+++ b/solution.py
@@ -691,7 +691,7 @@
         centre = jnp.mean(grad, axis=1, keepdims=True)
         along = jnp.mean(grad * unit, axis=1, keepdims=True)
         change = factor[block, pl.ds(0, 1)] * (grad - centre - unit * along)
-        out[block, :] = (gs[block, :].astype(f32) + change).astype(half)
+        out[block, :] = gs[block, :].astype(f32) + change
 
     for d in range(1, NZ):
         landed(from_z.at[d - 1], recv_z.at[d - 1])
@@ -817,7 +817,7 @@
     grad_nodes, grad_out_proj = pl.pallas_call(
         layer_kernel,
         out_shape=[
-            jax.ShapeDtypeStruct(full, half),
+            jax.ShapeDtypeStruct(full, f32),
             jax.ShapeDtypeStruct((own * NY, width // NY), f32),
         ],
         in_specs=[outside] * 10,
@@ -839,7 +839,7 @@
         target.reshape(rows, variables),
         node_area.reshape(1, rows),
     )
-    return grad_nodes.reshape(nodes.shape), grad_out_proj.reshape(-1)
+    return grad_nodes.astype(half).reshape(nodes.shape), grad_out_proj.reshape(-1)
 
 
 def solution(mesh):

time: 97.3 us -> 97.5 us (level)
  other arithmetic: 0 us -> 1.78 us
  local copies, waits for them, and re-layouts: 2.28 us -> 0.6 us
    reshape x0 -> x1, other arithmetic: none -> 1.78 us  [shards(): grad_nodes.astype(half).reshape(nodes.shape)]
    unnamed x4 -> x3, local copies, waits for them, and re-layouts: 2.28 us -> 0.6 us
where the time goes in v5:
time: 97.5 us; the launch traced here: 97.3 us
  Pallas kernels  94.3 us (97%)
  other arithmetic  1.78 us (2%)
    pallas_call x1, Pallas kernels, shards(): pl.pallas_call(layer_kernel, out_shape=[jax.ShapeDtypeStruct(full, f32),...  94.3 us

profile of v5, /device:TPU:1, one launch (start us, length us, event | category | flops | bytes accessed | tf_op | source)
XLA Modules:
  0.0 97.3 jit_solution(17735400822577388805)
XLA Ops:
  0.6 94.3 %layer.1 = (f32[128,1024]{1,0:T(8,128)}, f32[16,128]{1,0:T(8,128)}) custom-call(bf16[128,1024]{1,0:T(8,128)(2,1)} %bitcast.8, bf16[32,1024]{1,0:T(8,128)(2,1)} %wq_shard.1, bf16[32,1024]{1,0:T(8,128)(2,1)} %wk_shard.1, bf16[32,1024]{1,0:T(8,128)(2,1)} %wv_shard.1, bf16[32,1024]{1,0:T(8,128)(2,1)} %wo_shard.1, bf16[32,128]{1,0:T(8,128)(2,1)} %wh_shard.1, ...), custom_call_target="tpu_custom_call" | custom-call | tf_op jit(solution)/shard_map/layer/pallas_call | solution.py:817
  94.9 0.0 copy-start
  95.0 1.8 %convert_bitcast_fusion = bf16[1,1,128,1024]{3,2,1,0:T(8,128)(2,1)} fusion(f32[128,1024]{1,0:T(8,128)} %get-tuple-element.4), kind=kLoop, calls=%fused_computation | loop fusion | flops 131072 | bytes 786432 | tf_op jit(solution)/shard_map/reshape | solution.py:842
  96.7 0.0 copy-done
  96.7 0.6 copy.13
Async XLA Ops:
  94.9 1.8 %copy-start = (f32[16,128]{1,0:T(8,128)S(1)}, f32[16,128]{1,0:T(8,128)}, u32[]{:S(2)}) copy-start(f32[16,128]{1,0:T(8,128)} %get-tuple-element.5) | copy-start | bytes 24580
